TPU v7x, 256 devices: a whole 4x4x8 slice. The times are simulated.
256 devices in a mesh: dp: 64 (over x, y_lo, z), fsdp: 4 (over y_hi, core).
Axes of the slice: x: 4, y: 4 (y_hi: 2, y_lo: 2; y = y_hi * 2 + y_lo), z: 8, core: 2. Of those that a mesh axis runs over, the one named last changes fastest.
Arguments:
- frames: bfloat16 [64, 4, 48, 64, 128], P('dp', 'fsdp'), may hold values from -6 to 6
- occupied_slot_counts: int32 [4, 64], P('fsdp', 'dp'), may hold values from 1 to 48, 1024 in all within a row
- block_frame_rows: int32 [64, 4, 48], P('dp', 'fsdp'), may hold values from 1 to 16
- order: int32 [4, 64], P('fsdp'), may hold values from 0 to 63, each once within a row
- cotangent: bfloat16 [64, 4, 16, 16, 1536], P('dp', 'fsdp'), may hold values from -6 to 6
- sub_weight: bfloat16 [512, 1536], P('fsdp'), may hold values from -0.25 to 0.25
- depth_kernel: float32 [31, 1536], replicated, may hold values from -1 to 1
- norm_gain: float32 [1536], replicated, may hold values from 0.5 to 1.5
- w_in: bfloat16 [1536, 3072], P('fsdp'), may hold values from -0.15625 to 0.15625
- w_out: bfloat16 [3072, 1536], P('fsdp'), may hold values from -0.109375 to 0.109375
Outputs:
- grad_in: bfloat16 [64, 1536, 3072], P('dp', 'fsdp')
- grad_out: bfloat16 [64, 3072, 1536], P('dp', 'fsdp')
- kernel_grad: float32 [31, 1536], replicated
Inputs may be any that keep to these rules, and one draw needn't show every extreme that they name: `occupied_slot_counts`: for each fsdp index the 64 counts sum to 1024, and the largest is 48.
All inputs are finite; a program needn't handle non-finite values. No bound on the sum of `occupied_slot_counts` on one device may be relied on, other than what follows from the above.
Results may differ from a plain program's by a relative error of at most 0.02.
Values may be sent and summed in bfloat16 or wider, within the bound.
A program may use at most 128 MiB of HBM per device.

v0:
```python
import jax
import jax.numpy as jnp
from jax import lax
from jax.sharding import PartitionSpec as P

D = 1536
MEL = 128
BR = 16


EPSILON = 1e-05


def prefix(value, axis, join, neutral):
    count, mine = (lax.axis_size(axis), lax.axis_index(axis))
    pieces = lax.all_gather(value, axis)
    so_far = jnp.full_like(value, 0) + jnp.asarray(neutral, value.dtype)

    def turn(position, so_far):
        longer = join(so_far, pieces[position])
        return jnp.where(position < mine, longer, so_far)

    return lax.fori_loop(0, count - 1, turn, so_far)


def swish_slope(values):
    sigma = jax.nn.sigmoid(values)
    return sigma * (1.0 + values * (1.0 - sigma))


def layer_norm(mixed, norm_gain):
    mean_value = jnp.mean(mixed, axis=-1, keepdims=True)
    centred = mixed - mean_value
    variance = jnp.mean(centred * centred, axis=-1, keepdims=True)
    return centred * lax.rsqrt(variance + EPSILON) * norm_gain


def padded_blocks(features, tap_count):
    half_span = (tap_count - 1) // 2
    return jnp.pad(features, ((0, 0), (half_span, half_span), (0, 0)))


def depthwise(features, depth_kernel):
    tap_count = depth_kernel.shape[0]
    steps_len = features.shape[1]
    padded = padded_blocks(features, tap_count)
    running = jnp.zeros(features.shape, features.dtype)
    for tap_index in range(tap_count):
        running = (
            running + padded[:, tap_index : tap_index + steps_len, :] * depth_kernel[tap_index]
        )
    return running


def kernel_terms(conv_grad, features, tap_count):
    steps_len = features.shape[1]
    padded = padded_blocks(features, tap_count)
    columns = [
        jnp.sum(conv_grad * padded[:, tap_index : tap_index + steps_len, :], axis=(0, 1))
        for tap_index in range(tap_count)
    ]
    return jnp.stack(columns)


def contract(left, right, left_dim, right_dim):
    return lax.dot_general(
        left, right, (((left_dim,), (right_dim,)), ((), ())), preferred_element_type=jnp.float32
    )


def add_rows(left_rows, weight_piece):
    return jnp.dot(left_rows, weight_piece, preferred_element_type=jnp.float32)


def on_device(
    frames,
    occupied_slot_counts,
    block_frame_rows,
    order,
    cotangent,
    sub_weight,
    depth_kernel,
    norm_gain,
    w_in,
    w_out,
):
    dp_width = lax.axis_size("dp")
    home_blocks = frames[0, 0]
    home_rows = block_frame_rows[0, 0]
    ranking = order[0]
    live_count = occupied_slot_counts[0, 0]
    home_total = home_blocks.shape[0]
    earlier_total = prefix(
        occupied_slot_counts[0],
        "dp",
        lambda earlier, later: earlier + later,
        jnp.zeros((1,), jnp.int32),
    )[0]
    capacity = (home_total + dp_width - 1) // dp_width
    slot_total = dp_width * capacity
    home_index = jnp.arange(home_total, dtype=jnp.int32)
    global_index = earlier_total + home_index
    residue = global_index % dp_width
    target = jnp.sum(
        jnp.where(
            residue[:, None] == jnp.arange(dp_width, dtype=jnp.int32)[None, :], ranking[None, :], 0
        ),
        axis=1,
        dtype=jnp.int32,
    )
    send_slot = target * capacity + home_index // dp_width
    chosen = (home_index[None, :] < live_count) & (
        send_slot[None, :] == jnp.arange(slot_total, dtype=jnp.int32)[:, None]
    )
    packed = jnp.einsum(
        "sh,hfc->sfc", chosen.astype(jnp.bfloat16), home_blocks, preferred_element_type=jnp.float32
    ).astype(jnp.bfloat16)
    sent_any = jnp.any(chosen, axis=1)
    sent_place = jnp.where(
        sent_any,
        jnp.sum(jnp.where(chosen, (global_index // dp_width)[None, :], 0), axis=1, dtype=jnp.int32),
        -1,
    )
    sent_rows = jnp.sum(jnp.where(chosen, home_rows[None, :], 0), axis=1, dtype=jnp.int32)
    got_blocks, got_place, got_rows = (
        lax.all_to_all(packed, "dp", split_axis=0, concat_axis=0, tiled=True),
        lax.all_to_all(sent_place, "dp", split_axis=0, concat_axis=0, tiled=True),
        lax.all_to_all(sent_rows, "dp", split_axis=0, concat_axis=0, tiled=True),
    )
    block_total = cotangent.shape[2]
    placing = got_place[None, :] == jnp.arange(block_total, dtype=jnp.int32)[:, None]
    frame_blocks = jnp.einsum(
        "bs,sfc->bfc", placing.astype(jnp.bfloat16), got_blocks, preferred_element_type=jnp.float32
    ).astype(jnp.bfloat16)
    valid_row_counts = jnp.sum(jnp.where(placing, got_rows[None, :], 0), axis=1, dtype=jnp.int32)
    row_total = block_total * BR
    row_mask = (
        (jnp.arange(BR, dtype=jnp.int32)[None, :] < valid_row_counts[:, None])
        .astype(jnp.float32)
        .reshape(row_total, 1)
    )
    patches = frame_blocks.reshape(row_total, 4 * MEL)
    projected = add_rows(patches, lax.all_gather(sub_weight, "fsdp", axis=0, tiled=True))
    features = (projected * row_mask).astype(jnp.bfloat16)
    feature_blocks = (
        lax.optimization_barrier(features).astype(jnp.float32).reshape(block_total, BR, D)
    )
    block_mask = row_mask.reshape(block_total, BR, 1)
    conv_out = depthwise(feature_blocks, depth_kernel)
    mixed = feature_blocks + block_mask * conv_out * jax.nn.sigmoid(conv_out)
    mixed_rows = mixed.reshape(row_total, D)
    normed = layer_norm(mixed_rows, norm_gain).astype(jnp.bfloat16)
    whole_in = lax.all_gather(w_in, "fsdp", axis=0, tiled=True)
    pre_act = jnp.dot(normed, whole_in, preferred_element_type=jnp.float32)
    hidden = (pre_act * jax.nn.sigmoid(pre_act)).astype(jnp.bfloat16)
    masked_cot = jnp.where(
        row_mask > 0, cotangent[0, 0].reshape(row_total, D), jnp.zeros((), jnp.bfloat16)
    )
    hidden_grad = 0.5 * contract(
        masked_cot, lax.all_gather(w_out, "fsdp", axis=0, tiled=True), 1, 1
    )
    pre_grad = (hidden_grad * swish_slope(pre_act)).astype(jnp.bfloat16)
    normed_grad = contract(pre_grad, whole_in, 1, 1)
    norm_pullback = jax.vjp(lambda values: layer_norm(values, norm_gain), mixed_rows)[1]
    mixed_grad = masked_cot.astype(jnp.float32) + norm_pullback(normed_grad)[0]
    conv_grad = block_mask * mixed_grad.reshape(block_total, BR, D) * swish_slope(conv_out)
    kernel_part = kernel_terms(conv_grad, feature_blocks, depth_kernel.shape[0])
    grad_in = lax.psum_scatter(
        contract(normed, pre_grad, 0, 0).astype(jnp.bfloat16),
        "fsdp",
        scatter_dimension=0,
        tiled=True,
    )
    grad_out = lax.psum_scatter(
        (0.5 * contract(hidden, masked_cot, 0, 0)).astype(jnp.bfloat16),
        "fsdp",
        scatter_dimension=0,
        tiled=True,
    )
    kernel_grad = lax.psum(kernel_part, ("dp", "fsdp")) / row_total
    return (grad_in[None], grad_out[None], kernel_grad)


def solution(mesh):
    placed = (
        P("dp", "fsdp", None, None, None),
        P("fsdp", "dp"),
        P("dp", "fsdp", None),
        P("fsdp", None),
        P("dp", "fsdp", None, None, None),
        P("fsdp", None),
        P(),
        P(),
        P("fsdp", None),
        P("fsdp", None),
    )
    return jax.shard_map(
        on_device,
        mesh=mesh,
        in_specs=placed,
        out_specs=(P("dp", "fsdp", None), P("dp", "fsdp", None), P()),
        check_vma=False,
    )
```

profile of v0, /device:TPU:1, one launch (start us, length us, event | category | flops | bytes accessed | tf_op | source)
XLA Modules:
  0.0 657.2 jit_solution(13325077425364818482)
XLA Ops:
  11.3 22.8 %all-reduce.1 = s32[64]{0:T(128)S(1)} all-reduce(s32[64]{0:T(128)S(1)} %bitcast_dynamic-update-slice_fusion), channel_id=1, replica_groups=mesh['dp'=64,'fsdp'=4] {'dp'}, use_global_device_ids=true, to_apply=%add.1 | all-reduce | flops 64 | bytes 512
  34.0 78.4 %while.13 = (s32[]{:T(128)}, s32[1]{0:T(128)}, s32[]{:T(128)}, s32[64,1]{0,1:T(1,128)S(1)}, s32[]{:T(128)}) while((s32[]{:T(128)}, s32[1]{0:T(128)}, s32[]{:T(128)}, s32[64,1]{0,1:T(1,128)S(1)}, s32[]{:T(128)}) %tuple.111), condition=%wide.region_1.2_spmd, body=%wide.region_0.1_spmd.sunk | while | flops 5 | bytes 115 | solution.py:23
  112.9 0.7 copy.26
  113.6 4.6 all-to-all-start
  118.9 8.5 %all-to-all-done = s32[64,1,1]{2,1,0:T(1,128)S(1)} async-done(((s32[64,1,1]{2,1,0:T(1,128)}), s32[64,1,1]{2,1,0:T(1,128)S(1)}, u32[]{:S(2)}, u32[]{:S(2)}) %all-to-all-start) | async-done | bytes 288 | tf_op jit(solution)/shard_map/all_to_all | solution.py:127
  127.4 4.6 all-to-all-start.2
  132.0 0.8 convolution_convert_fusion.1
  132.8 1.6 copy.28
  134.5 6.7 %all-to-all-done.2 = s32[64,1,1]{2,1,0:T(1,128)S(1)} async-done(((s32[64,1,1]{2,1,0:T(1,128)}), s32[64,1,1]{2,1,0:T(1,128)S(1)}, u32[]{:S(2)}, u32[]{:S(2)}) %all-to-all-start.2) | async-done | bytes 288 | tf_op jit(solution)/shard_map/all_to_all | solution.py:128
  141.2 4.7 all-to-all-start.1
  146.5 1.2 reduce.2
  147.7 1.2 reduce.3
  149.2 1.1 bitcast_select_fusion
  150.3 14.3 %all-to-all-done.1 = bf16[64,64,128]{2,1,0:T(8,128)(2,1)S(1)} async-done(((bf16[64,64,128]{2,1,0:T(8,128)(2,1)}), bf16[64,64,128]{2,1,0:T(8,128)(2,1)S(1)}, u32[]{:S(2)}, u32[]{:S(2)}) %all-to-all-start.1) | async-done | bytes 1048608 | tf_op jit(solution)/shard_map/all_to_all | solution.py:126
  165.6 2.0 fusion.2
  167.7 6.5 multiply_add_fusion
  174.9 1.2 multiply_convert_fusion.3
  176.1 8.2 %fusion.19 = f32[256,3072]{1,0:T(8,128)} fusion(bf16[256,1536]{1,0:T(8,128)(2,1)} %multiply_convert_fusion.3, bf16[1536,3072]{1,0:T(8,128)(2,1)} %all-gather.8.cloned.1.call-done), kind=kOutput, calls=%fused_computation.158 | convolution fusion | flops 2415919104 | bytes 13369344 | tf_op jit(solution)/shard_map/dot_general | solution.py:154
  184.3 12.0 %all-gather.6.cloned.1.call-done = bf16[3072,1536]{1,0:T(8,128)(2,1)} async-done(((bf16[768,1536]{1,0:T(8,128)(2,1)}), bf16[3072,1536]{1,0:T(8,128)(2,1)}) %all-gather.6.cloned.1.call-update) | async-done | bytes 9437200 | tf_op jit(solution)/shard_map/all_gather | solution.py:160
  196.3 7.7 %fusion.1 = bf16[256,3072]{1,0:T(8,128)(2,1)S(1)} fusion(bf16[256,1536]{1,0:T(8,128)(2,1)} %bitcast_select_fusion, bf16[3072,1536]{1,0:T(8,128)(2,1)} %all-gather.6.cloned.1.call-done, f32[256,3072]{1,0:T(8,128)} %fusion.19), kind=kOutput, calls=%fused_computation.35 | convolution fusion | flops 2423783424 | bytes 14942208 | tf_op jit(solution)/shard_map/dot_general | solution.py:66
  204.0 2.9 multiply_reduce_fusion.31
  207.4 0.9 copy-done.4
  208.5 4.9 multiply_reduce_fusion
  213.5 2.6 multiply_reduce_fusion.19
  216.5 2.8 stack.127
  219.3 8.4 %multiply_convert_fusion = bf16[3072,1536]{1,0:T(8,128)(2,1)} fusion(bf16[256,1536]{1,0:T(8,128)(2,1)S(1)} %copy-done.10, f32[256,3072]{1,0:T(8,128)} %fusion.19), kind=kOutput, calls=%fused_computation.31 | convolution fusion | flops 2429288448 | bytes 13369344 | tf_op jit(solution)/shard_map/dot_general | solution.py:66
  227.8 1.1 copy-done.5
  229.4 5.1 convolution_convert_fusion
  234.5 230.0 %all-reduce.4.cloned.1.call-done = f32[31,1536]{1,0:T(8,128)} async-done(((f32[31,1536]{1,0:T(8,128)}), f32[31,1536]{1,0:T(8,128)}) %all-reduce.4.cloned.1.call-update) | async-done | bytes 190480 | tf_op jit(solution)/shard_map/psum | solution.py:180
  464.5 1.6 broadcast_multiply_fusion
  466.1 90.9 %reduce-scatter.5.cloned.1.call-done = bf16[768,1536]{1,0:T(8,128)(2,1)} async-done(((bf16[3072,1536]{1,0:T(8,128)(2,1)}), bf16[768,1536]{1,0:T(8,128)(2,1)}) %reduce-scatter.5.cloned.1.call-update) | async-done | bytes 2359312 | tf_op jit(solution)/shard_map/reduce_scatter | solution.py:174
  557.1 93.2 %reduce-scatter.3.cloned.1.call-done = bf16[384,3072]{1,0:T(8,128)(2,1)} async-done(((bf16[1536,3072]{1,0:T(8,128)(2,1)}), bf16[384,3072]{1,0:T(8,128)(2,1)}) %reduce-scatter.3.cloned.1.call-update) | async-done | bytes 2359312 | tf_op jit(solution)/shard_map/reduce_scatter | solution.py:168
  (171 shorter events, 46.0 us)
Async XLA Ops:
  7.2 124.9 %copy-start = (bf16[1,1,48,64,128]{4,3,2,1,0:T(8,128)(2,1)S(1)}, bf16[1,1,48,64,128]{4,3,2,1,0:T(8,128)(2,1)}, u32[]{:S(2)}) copy-start(bf16[1,1,48,64,128]{4,3,2,1,0:T(8,128)(2,1)} %param.12) | copy-start | bytes 2359300
  7.2 158.4 %all-gather.4.cloned.1.call-start = ((), (), s32[]{:S(2)}) async-start(), calls=%async_computation.5 | async-start | bytes 1966080 | tf_op jit(solution)/shard_map/all_gather | solution.py:143
  7.9 168.2 %all-gather.8.cloned.1.call-start = ((), (), s32[]{:S(2)}) async-start(), calls=%async_computation.7 | async-start | bytes 11796480 | tf_op jit(solution)/shard_map/all_gather | solution.py:153
  8.7 1.4 copy-start.16
  8.7 103.8 %copy-start.15 = (s32[1,64]{1,0:T(1,128)S(1)}, s32[1,64]{1,0:T(1,128)}, u32[]{:S(2)}) copy-start(s32[1,64]{1,0:T(1,128)} %param.15) | copy-start | bytes 772
  8.7 104.1 %copy-start.13 = (s32[1,1,48]{2,1,0:T(1,128)S(1)}, s32[1,1,48]{2,1,0:T(1,128)}, u32[]{:S(2)}) copy-start(s32[1,1,48]{2,1,0:T(1,128)} %param.14) | copy-start | bytes 580
  8.7 187.6 %all-gather.6.cloned.1.call-start = ((), (), s32[]{:S(2)}) async-start(), calls=%async_computation.6 | async-start | bytes 11796480 | tf_op jit(solution)/shard_map/all_gather | solution.py:160
  113.6 13.8 %all-to-all-start = ((s32[64,1,1]{2,1,0:T(1,128)}), s32[64,1,1]{2,1,0:T(1,128)S(1)}, u32[]{:S(2)}, u32[]{:S(2)}) async-start(s32[64,1,1]{2,1,0:T(1,128)} %copy.26), calls=%async_computation | async-start | bytes 65536 | tf_op jit(solution)/shard_map/all_to_all | solution.py:127
  127.4 13.8 %all-to-all-start.2 = ((s32[64,1,1]{2,1,0:T(1,128)}), s32[64,1,1]{2,1,0:T(1,128)S(1)}, u32[]{:S(2)}, u32[]{:S(2)}) async-start(s32[64,1,1]{2,1,0:T(1,128)} %copy.31), calls=%async_computation.2 | async-start | bytes 65536 | tf_op jit(solution)/shard_map/all_to_all | solution.py:128
  132.8 13.1 %copy-start.11 = (f32[31,1536]{1,0:T(8,128)S(1)}, f32[31,1536]{1,0:T(8,128)}, u32[]{:S(2)}) copy-start(f32[31,1536]{1,0:T(8,128)} %param.18) | copy-start | bytes 571396
  134.5 14.7 %copy-start.6 = (bf16[1,1,16,16,1536]{4,3,2,1,0:T(8,128)(2,1)S(1)}, bf16[1,1,16,16,1536]{4,3,2,1,0:T(8,128)(2,1)}, u32[]{:S(2)}) copy-start(bf16[1,1,16,16,1536]{4,3,2,1,0:T(8,128)(2,1)} %param.16) | copy-start | bytes 2359300
  141.2 23.4 %all-to-all-start.1 = ((bf16[64,64,128]{2,1,0:T(8,128)(2,1)}), bf16[64,64,128]{2,1,0:T(8,128)(2,1)S(1)}, u32[]{:S(2)}, u32[]{:S(2)}) async-start(bf16[64,64,128]{2,1,0:T(8,128)(2,1)} %copy.28), calls=%async_computation.1 | async-start | bytes 2097152 | tf_op jit(solution)/shard_map/all_to_all | solution.py:126
  145.9 318.6 %all-reduce.4.cloned.1.call-start = ((), (), s32[]{:S(2)}) async-start(), calls=%async_computation.10 | async-start | bytes 393216 | tf_op jit(solution)/shard_map/psum | solution.py:180
  167.5 6.7 %copy-start.2 = (bf16[256,1536]{1,0:T(8,128)(2,1)}, bf16[256,1536]{1,0:T(8,128)(2,1)S(1)}, u32[]{:S(2)}) copy-start(bf16[256,1536]{1,0:T(8,128)(2,1)S(1)} %fusion.2) | copy-start | bytes 2359300
  174.2 0.7 copy-start.12
  196.3 7.7 %copy-start.14 = (bf16[1536,3072]{1,0:T(8,128)(2,1)S(1)}, bf16[1536,3072]{1,0:T(8,128)(2,1)}, u32[]{:S(2)}) copy-start(bf16[1536,3072]{1,0:T(8,128)(2,1)} %all-gather.8.cloned.1.call-done) | copy-start | bytes 28311556
  204.0 2.9 copy-start.8
  206.9 1.4 copy-start.4
  206.9 1.6 copy-start.7
  208.5 5.0 copy-start.3
  213.5 5.8 copy-start.10
  219.3 337.8 %reduce-scatter.5.cloned.1.call-start = ((), (), s32[]{:S(2)}) async-start(), calls=%async_computation.9 | async-start | bytes 11796480 | tf_op jit(solution)/shard_map/reduce_scatter | solution.py:174
  227.8 1.1 copy-start.5
  227.8 1.7 copy-start.9
  227.8 422.5 %reduce-scatter.3.cloned.1.call-start = ((), (), s32[]{:S(2)}) async-start(), calls=%async_computation.8 | async-start | bytes 11796480 | tf_op jit(solution)/shard_map/reduce_scatter | solution.py:168
  234.5 415.8 %copy-start.1 = (bf16[1,1,48,64,128]{4,3,2,1,0:T(8,128)(2,1)S(1)}, bf16[1,1,48,64,128]{4,3,2,1,0:T(8,128)(2,1)}, u32[]{:S(2)}) copy-start(bf16[1,1,48,64,128]{4,3,2,1,0:T(8,128)(2,1)} %param.12) | copy-start | bytes 2359300
Sparse Core Ops, SparseCore 0:
  9.8 30.5 all-gather.3
  42.2 70.2 all-gather.7
  114.3 81.9 all-gather.5
  219.4 245.0 all-reduce.3
  467.8 89.2 reduce-scatter.4
  560.3 89.9 reduce-scatter.2
where the time goes:
time: 660 us; the launch traced here: 657 us
  waiting for transfers between devices  458 us (69%)
  local copies, waits for them, and re-layouts  48.3 us (7%)
  loops' own time  41.1 us (6%)
  matrix products  35.7 us (5%)
  blocking collectives  22.8 us (3%)
  other arithmetic  22 us (3%)
  between operations  15.4 us (2%)
  starting transfers between devices  14.1 us (2%)
    psum x1, waiting for transfers between devices, on_device(): kernel_grad = lax.psum(kernel_part, ('dp', 'fsdp')) / row_total  230 us
    reduce_scatter x1, waiting for transfers between devices, on_device(): lax.psum_scatter(contract(normed, pre_grad, 0, 0).astype(jnp.bfloat16), '...  93.2 us
    reduce_scatter x1, waiting for transfers between devices, on_device(): lax.psum_scatter((0.5 * contract(hidden, masked_cot, 0, 0)).astype(jnp.bf...  90.9 us
    another operation x1, loops' own time, prefix(): return lax.fori_loop(0, count - 1, turn, so_far)  41.1 us
    dynamic_slice x63, local copies, waits for them, and re-layouts, turn(): longer = join(so_far, pieces[position])  37.3 us
    dot_general x4, matrix products, contract(): lax.dot_general(left, right, (((left_dim,), (right_dim,)), ((), ())), pre...  24 us
    unnamed x1, blocking collectives  22.8 us
    all_to_all x1, waiting for transfers between devices, on_device(): lax.all_to_all(packed, 'dp', split_axis=0, concat_axis=0, tiled=True)  14.3 us
  transfers between devices with their start and end apart: 9, of which 7 were waited for; matrix products, arithmetic and copies ran while one was open for 12% of the time, Pallas kernels for 0%

commit v1 on v0

v1 whole, which is shorter than its diff:
```python
import functools

import jax
import jax.numpy as jnp
from jax import lax
from jax.experimental import pallas as pl
from jax.experimental.pallas import tpu as pltpu
from jax.sharding import PartitionSpec as P

D = 1536
FF = 3072
K = 31
BR = 16
NB = 16
NH = 48
NDP = 64
ROWS = NB * BR
HALF = FF // 2
FSH = FF // 4
DSH = D // 4
SSH = 128
EPSILON = 1e-05
MESH = pl.DeviceIdType.MESH
F32 = jnp.float32
BF16 = jnp.bfloat16
VLIM = 60 * 1024 * 1024

ANY = pl.BlockSpec(memory_space=pl.ANY)
VM = pl.BlockSpec(memory_space=pltpu.VMEM)
SM = pl.BlockSpec(memory_space=pltpu.SMEM)


def place():
    dp, f = lax.axis_index("dp"), lax.axis_index("fsdp")
    return dp, f, dp // 16, (dp // 8) % 2, dp % 8, f // 2, f % 2


def dev(x, yl, z, yh, c):
    return ((x * 2 + yl) * 8 + z, yh * 2 + c)


def greet(peers, extra=0):
    bar = pltpu.get_barrier_semaphore()
    for peer in peers:
        pl.semaphore_signal(bar, inc=1, device_id=peer, device_id_type=MESH)
    pl.semaphore_wait(bar, len(peers) + extra)


def remote(src, dst, send, recv, device):
    return pltpu.make_async_remote_copy(
        src_ref=src, dst_ref=dst, send_sem=send, recv_sem=recv, device_id=device, device_id_type=MESH
    )


class Sent:
    def __init__(self, src, dst, ss, rs, i, device):
        self.sems, self.device = (ss.at[i], rs.at[i]), device
        self.copy = remote(src, dst, *self.sems, device)

    def start(self):
        self.copy.start()

    def wait(self):
        self.copy.wait()

    def wait_send(self):
        self.copy.wait_send()

    def wait_got(self, ref):
        remote(ref, ref, *self.sems, self.device).wait_recv()


def meta_kernel(mine, table, ss, rs, gs, gr):
    dp, f, x, yl, z, yh, c = place()
    mates = [(dp, yh * 2 + 1 - c), (dp, (1 - yh) * 2 + c), (dp, (1 - yh) * 2 + 1 - c)]
    bar = pltpu.get_barrier_semaphore()

    def signal(k, carry):
        pl.semaphore_signal(bar, inc=1, device_id=(lax.rem(dp + k, NDP), f), device_id_type=MESH)
        return carry

    lax.fori_loop(1, NDP, signal, 0)
    greet(mates, NDP - 1)
    table[pl.ds(f * NDP, 1)] = mine[...]

    def send(k, carry):
        to = lax.rem(dp + k, NDP)
        row = pl.ds(f * NDP + k, 1)
        remote(mine, table.at[row], ss, rs, (to, f)).start()
        return carry

    lax.fori_loop(1, NDP, send, 0)
    rest = table.at[pl.ds(f * NDP + 1, NDP - 1)]
    remote(rest, rest, ss, rs, mates[0]).wait()
    whole = table.at[pl.ds(f * NDP, NDP)]
    copies = [remote(whole, whole, gs.at[i], gr.at[i], mate) for i, mate in enumerate(mates)]
    for copy in copies:
        copy.start()
    for copy in copies:
        copy.wait()


def group_table(mine):
    return pl.pallas_call(
        meta_kernel,
        out_shape=jax.ShapeDtypeStruct((4 * NDP, 1, 128), jnp.int32),
        in_specs=[VM],
        out_specs=VM,
        scratch_shapes=[
            pltpu.SemaphoreType.DMA,
            pltpu.SemaphoreType.DMA,
            pltpu.SemaphoreType.DMA((3,)),
            pltpu.SemaphoreType.DMA((3,)),
        ],
        compiler_params=pltpu.CompilerParams(collective_id=1, has_side_effects=True),
        name="group_table",
    )(mine)


def move_kernel(
    hsel, slot, frames, cot, w_in, w_out, sub,
    blocks, cots, winh, wouth, suba, stage,
    sbuf, rbuf, as_, ar, ss, rs, ls,
):
    dp, f, x, yl, z, yh, c = place()
    fo, fs, fso = (1 - yh) * 2 + c, yh * 2 + 1 - c, (1 - yh) * 2 + 1 - c
    color = lax.rem(x + 2 * z, 4)
    across = dev(x, 1 - yl, z, 1 - yh, c)
    other = (dp, fo)
    sibling = (dp, fs)
    xp, xm = dev(lax.rem(x + 1, 4), yl, z, yh, c), dev(lax.rem(x + 3, 4), yl, z, yh, c)
    zp, zm = dev(x, yl, lax.rem(z + 1, 8), yh, c), dev(x, yl, lax.rem(z + 7, 8), yh, c)
    bar = pltpu.get_barrier_semaphore()

    def signal(k, carry):
        pl.semaphore_signal(bar, inc=1, device_id=(lax.rem(dp + k, NDP), f), device_id_type=MESH)
        return carry

    lax.fori_loop(1, NDP, signal, 0)
    greet([across, other, sibling], NDP - 1)

    count = iter(range(64))

    def rcopy(src, dst, device):
        return Sent(src, dst, ss, rs, next(count), device)

    def cols(g):
        return pl.ds(pl.multiple_of(g * FSH, FSH), FSH)

    def rows(start, size):
        return pl.ds(pl.multiple_of(start, 16), size)

    lo, hi = pl.ds(0, FSH), pl.ds(FSH, FSH)
    q = rows(color * (DSH // 4), DSH // 4)
    qd = rows(f * DSH + color * (DSH // 4), DSH // 4)
    y_sub = [rcopy(sub.at[rows(color * 32, 32)], suba.at[rows(f * SSH + color * 32, 32)], across)]
    y_out = [rcopy(w_out.at[rows(color * 192, 192)], wouth.at[rows(FSH + color * 192, 192)], across)]
    y_in = [
        rcopy(w_in.at[q, cols(fo)], winh.at[qd, lo], across),
        rcopy(w_in.at[q, cols(f)], winh.at[qd, hi], across),
        rcopy(w_in.at[q, cols(fso)], stage.at[q, lo], across),
        rcopy(w_in.at[q, cols(fs)], stage.at[q, hi], across),
    ]
    for copy in y_sub + y_out + y_in:
        copy.start()
    cot_other = rcopy(cot, cots.at[1], other)
    cot_other.start()
    mine = rows(f * DSH, DSH)
    on_chip = [
        rcopy(sub, suba.at[rows(f * SSH, SSH)], sibling),
        rcopy(cot, cots.at[2], sibling),
        rcopy(w_in.at[:, cols(fs)], winh.at[mine, lo], sibling),
        rcopy(w_in.at[:, cols(fso)], winh.at[mine, hi], sibling),
    ]
    local = [
        pltpu.make_async_copy(cot, cots.at[0], ls.at[0]),
        pltpu.make_async_copy(sub, suba.at[rows(f * SSH, SSH)], ls.at[1]),
        pltpu.make_async_copy(w_out, wouth.at[pl.ds(0, FSH)], ls.at[2]),
        pltpu.make_async_copy(w_in.at[:, cols(f)], winh.at[mine, lo], ls.at[3]),
        pltpu.make_async_copy(w_in.at[:, cols(fo)], winh.at[mine, hi], ls.at[4]),
    ]
    for copy in on_chip + local:
        copy.start()

    def pack(j, carry):
        sbuf[j] = frames[hsel[j]]
        return carry

    lax.fori_loop(0, NDP, pack, 0)

    def send(k, carry):
        to = lax.rem(dp + k, NDP)
        remote(sbuf.at[to], rbuf.at[k], as_, ar, (to, f)).start()
        return carry

    lax.fori_loop(1, NDP, send, 0)
    rbuf[0] = sbuf[dp]

    def forward(ref, start, size):
        a = start + color * size
        full, first, second = rows(a, size), rows(a, size // 2), rows(a + size // 2, size // 2)
        copies = [
            rcopy(ref.at[full], ref.at[full], xp),
            rcopy(ref.at[full], ref.at[full], xm),
            rcopy(ref.at[first], ref.at[first], zp),
            rcopy(ref.at[second], ref.at[second], zm),
        ]
        for copy in copies:
            copy.start()
        left, right = start + lax.rem(color + 3, 4) * size, start + lax.rem(color + 1, 4) * size
        far = start + lax.rem(color + 2, 4) * size
        spots = [rows(left, size), rows(right, size), rows(far, size // 2), rows(far + size // 2, size // 2)]
        return [(copy, ref.at[spot]) for copy, spot in zip(copies, spots)]

    y_sub[0].wait_send()
    y_sub[0].wait_got(suba.at[rows(fo * SSH + color * 32, 32)])
    arrive_sub = forward(suba, fo * SSH, 32)
    y_out[0].wait()
    arrive_out = forward(wouth, FSH, 192)
    for copy in y_in:
        copy.wait_send()
    qi = rows(fo * DSH + color * (DSH // 4), DSH // 4)
    for copy, ref in zip(y_in, [winh.at[qi, lo], winh.at[qi, hi], stage.at[q, lo], stage.at[q, hi]]):
        copy.wait_got(ref)
    arrive_in = forward(winh, fo * DSH, DSH // 4)
    arrive_stage = forward(stage, 0, DSH // 4)

    every = rbuf.at[pl.ds(1, NDP - 1)]
    remote(every, every, as_, ar, other).wait()

    def select(m, carry):
        blocks[m] = rbuf[slot[m]]
        return carry

    lax.fori_loop(0, NB, select, 0)
    fwd_blocks = rcopy(blocks.at[pl.ds(0, NB)], blocks.at[pl.ds(NB, NB)], other)
    fwd_blocks.start()

    def settle(pairs):
        for copy, ref in pairs:
            copy.wait_send()
        for copy, ref in pairs:
            copy.wait_got(ref)

    settle(arrive_sub)
    theirs = suba.at[rows(fo * SSH, SSH)]
    sub_sib = rcopy(theirs, theirs, sibling)
    sub_sib.start()
    cot_other.wait()
    cot_sib = rcopy(cots.at[1], cots.at[3], sibling)
    cot_sib.start()
    settle(arrive_out)
    settle(arrive_in)
    settle(arrive_stage)
    stage_sib = rcopy(stage, winh.at[rows(fo * DSH, DSH)], sibling)
    stage_sib.start()
    for copy in on_chip:
        copy.wait_send()
    for ref, copy in zip(
        [suba.at[rows(fs * SSH, SSH)], cots.at[2], winh.at[rows(fs * DSH, DSH), lo], winh.at[rows(fs * DSH, DSH), hi]],
        on_chip,
    ):
        copy.wait_got(ref)
    for copy in local:
        copy.wait()
    fwd_blocks.wait()
    sub_sib.wait_send()
    sub_sib.wait_got(suba.at[rows(fso * SSH, SSH)])
    cot_sib.wait()
    stage_sib.wait_send()
    stage_sib.wait_got(winh.at[rows(fso * DSH, DSH)])


def move(hsel, slot, frames, cot, w_in, w_out, sub):
    return pl.pallas_call(
        move_kernel,
        out_shape=[
            jax.ShapeDtypeStruct((2 * NB, 64, 128), BF16),
            jax.ShapeDtypeStruct((4, ROWS, D), BF16),
            jax.ShapeDtypeStruct((D, HALF), BF16),
            jax.ShapeDtypeStruct((HALF, D), BF16),
            jax.ShapeDtypeStruct((4 * SSH, D), BF16),
            jax.ShapeDtypeStruct((DSH, HALF), BF16),
        ],
        in_specs=[SM, SM, VM, ANY, ANY, ANY, ANY],
        out_specs=[VM, ANY, ANY, ANY, ANY, ANY],
        scratch_shapes=[
            pltpu.VMEM((NDP, 64, 128), BF16),
            pltpu.VMEM((NDP, 64, 128), BF16),
            pltpu.SemaphoreType.DMA,
            pltpu.SemaphoreType.DMA,
            pltpu.SemaphoreType.DMA((32,)),
            pltpu.SemaphoreType.DMA((32,)),
            pltpu.SemaphoreType.DMA((5,)),
        ],
        compiler_params=pltpu.CompilerParams(collective_id=2, has_side_effects=True),
        name="move",
    )(hsel, slot, frames, cot, w_in, w_out, sub)


def front_kernel(blocks, suba, cots, masks, taps, gain, masked, feat, conv, normed, ftmp):
    r = lax.broadcasted_iota(jnp.int32, (ROWS, ROWS), 0)
    col = lax.broadcasted_iota(jnp.int32, (ROWS, ROWS), 1)
    turn = jnp.where(col == lax.rem(r, NB) * BR + r // NB, 1.0, 0.0).astype(BF16)
    for g in range(4):
        mask = masks[g] > 0
        moved = jnp.dot(turn, cots[g], preferred_element_type=F32)
        masked[g] = jnp.where(mask, moved, 0.0).astype(BF16)
    r = lax.broadcasted_iota(jnp.int32, (ROWS, 4 * ROWS), 0)
    col = lax.broadcasted_iota(jnp.int32, (ROWS, 4 * ROWS), 1)
    want = lax.rem(r, NB) * (4 * BR) + 4 * (r // NB)
    for g in range(2):
        mask = masks[g]
        frames = blocks[pl.ds(g * NB, NB)].reshape(4 * ROWS, 128)
        total = jnp.zeros((ROWS, D), F32)
        for k in range(4):
            pick = jnp.where(col == want + k, 1.0, 0.0).astype(BF16)
            patch = jnp.dot(pick, frames, preferred_element_type=F32).astype(BF16)
            total += jnp.dot(patch, suba[pl.ds(k * 128, 128)], preferred_element_type=F32)
        feat[g] = (total * mask).astype(BF16)

        def chunk(l, carry):
            lanes = pl.ds(pl.multiple_of(l * 128, 128), 128)
            rows = [feat[g, pl.ds(t * NB, NB), lanes].astype(F32) for t in range(BR)]
            for t in range(BR):
                acc = None
                for s in range(BR):
                    tap = taps[pl.ds(s - t + 15, 1), lanes]
                    term = rows[s] * tap
                    acc = term if acc is None else acc + term
                if g == 0:
                    conv[pl.ds(t * NB, NB), lanes] = acc
                ftmp[pl.ds(t * NB, NB), lanes] = rows[t] + masks[g, pl.ds(t * NB, NB)] * (acc * jax.nn.sigmoid(acc))
            return carry

        lax.fori_loop(0, D // 128, chunk, 0)
        mixed = ftmp[...]
        mean = jnp.mean(mixed, axis=-1, keepdims=True)
        centred = mixed - mean
        variance = jnp.mean(centred * centred, axis=-1, keepdims=True)
        normed[g] = (centred * lax.rsqrt(variance + EPSILON) * gain[...]).astype(BF16)


def front(blocks, suba, cots, masks, taps, gain):
    return pl.pallas_call(
        front_kernel,
        out_shape=[
            jax.ShapeDtypeStruct((4, ROWS, D), BF16),
            jax.ShapeDtypeStruct((2, ROWS, D), BF16),
            jax.ShapeDtypeStruct((ROWS, D), F32),
            jax.ShapeDtypeStruct((2, ROWS, D), BF16),
        ],
        in_specs=[VM] * 6,
        out_specs=[VM] * 4,
        scratch_shapes=[pltpu.VMEM((ROWS, D), F32)],
        compiler_params=pltpu.CompilerParams(vmem_limit_bytes=VLIM),
        name="front",
    )(blocks, suba, cots, masks, taps, gain)


def nt(left, right):
    return lax.dot_general(left, right, (((1,), (1,)), ((), ())), preferred_element_type=F32)


def tn(left, right):
    return lax.dot_general(left, right, (((0,), (0,)), ((), ())), preferred_element_type=F32)


def middle_kernel(normed, masked, winh, wouth, nall, pgrad, hidden, ngrad, part, got, ss, rs):
    dp, f, x, yl, z, yh, c = place()
    sibling = (dp, yh * 2 + 1 - c)
    greet([sibling])
    swaps = [remote(normed.at[g], nall.at[2 + g], ss.at[g], rs.at[g], sibling) for g in range(2)]
    for swap in swaps:
        swap.start()
    nall[0] = normed[0]
    nall[1] = normed[1]

    def group(g):
        def tile(n, carry):
            w = pl.ds(pl.multiple_of(n * 256, 256), 256)
            pre = jnp.dot(nall[g], winh[:, w], preferred_element_type=F32)
            hgrad = 0.5 * nt(masked[g], wouth[w, :])
            sig = jax.nn.sigmoid(pre)
            hidden[g, :, w] = (pre * sig).astype(BF16)
            pgrad[g, :, w] = (hgrad * (sig * (1.0 + pre * (1.0 - sig)))).astype(BF16)
            return carry

        lax.fori_loop(0, HALF // 256, tile, 0)

    def back(g, ref):
        def tile(n, carry):
            w = pl.ds(pl.multiple_of(n * 256, 256), 256)
            ref[:, w] = nt(pgrad[g], winh[w, :])
            return carry

        lax.fori_loop(0, D // 256, tile, 0)

    group(0)
    swaps[0].wait()
    group(2)
    back(2, part)
    give = remote(part, got, ss.at[2], rs.at[2], sibling)
    give.start()
    back(0, ngrad)
    group(1)
    swaps[1].wait()
    group(3)
    give.wait()
    ngrad[...] += got[...]


def middle(normed, masked, winh, wouth):
    return pl.pallas_call(
        middle_kernel,
        out_shape=[
            jax.ShapeDtypeStruct((4, ROWS, D), BF16),
            jax.ShapeDtypeStruct((4, ROWS, HALF), BF16),
            jax.ShapeDtypeStruct((4, ROWS, HALF), BF16),
            jax.ShapeDtypeStruct((ROWS, D), F32),
        ],
        in_specs=[VM] * 4,
        out_specs=[VM] * 4,
        scratch_shapes=[
            pltpu.VMEM((ROWS, D), F32),
            pltpu.VMEM((ROWS, D), F32),
            pltpu.SemaphoreType.DMA((3,)),
            pltpu.SemaphoreType.DMA((3,)),
        ],
        compiler_params=pltpu.CompilerParams(collective_id=3, has_side_effects=True, vmem_limit_bytes=VLIM),
        name="middle",
    )(normed, masked, winh, wouth)


def taps_kernel(ngrad, masked, feat, conv, masks, gain, out, dmix):
    mask = masks[0]
    pre = conv[...]
    mixed = feat[0].astype(F32) + mask * (pre * jax.nn.sigmoid(pre))
    mean = jnp.mean(mixed, axis=-1, keepdims=True)
    centred = mixed - mean
    scale = lax.rsqrt(jnp.mean(centred * centred, axis=-1, keepdims=True) + EPSILON)
    hat = centred * scale
    dn = ngrad[...] * gain[...]
    m1 = jnp.mean(dn, axis=-1, keepdims=True)
    m2 = jnp.mean(dn * hat, axis=-1, keepdims=True)
    total = masked[0].astype(F32) + scale * (dn - m1 - hat * m2)
    sig = jax.nn.sigmoid(pre)
    dmix[...] = mask * total * (sig * (1.0 + pre * (1.0 - sig)))

    def chunk(l, carry):
        lanes = pl.ds(pl.multiple_of(l * 128, 128), 128)
        frows = [feat[0, pl.ds(s * NB, NB), lanes].astype(F32) for s in range(BR)]
        sums = [None] * K
        for t in range(BR):
            g = dmix[pl.ds(t * NB, NB), lanes]
            for s in range(BR):
                term = g * frows[s]
                k = s - t + 15
                sums[k] = term if sums[k] is None else sums[k] + term
        for k in range(K):
            out[l, pl.ds(k, 1), :] = jnp.sum(sums[k], axis=0, keepdims=True)
        out[l, pl.ds(K, 1), :] = jnp.zeros((1, 128), F32)
        return carry

    lax.fori_loop(0, D // 128, chunk, 0)


def tap_terms(ngrad, masked, feat, conv, masks, gain):
    return pl.pallas_call(
        taps_kernel,
        out_shape=jax.ShapeDtypeStruct((D // 128, K + 1, 128), F32),
        in_specs=[VM] * 6,
        out_specs=VM,
        scratch_shapes=[pltpu.VMEM((ROWS, D), F32)],
        compiler_params=pltpu.CompilerParams(vmem_limit_bytes=VLIM),
        name="tap_terms",
    )(ngrad, masked, feat, conv, masks, gain)


def last_kernel(part, nall, pgrad, hidden, masked, gin, gout, ktot, r1, s1, r2, s2, r3, give, ss, rs, gs, gr):
    dp, f, x, yl, z, yh, c = place()
    y = yh * 2 + yl
    near, far = z * 2 + c, x * 4 + y
    fo, fs = (1 - yh) * 2 + c, yh * 2 + 1 - c

    def near_dev(i):
        return dev(x, yl, i // 2, yh, lax.rem(i, 2))

    def far_dev(i):
        return dev(i // 4, lax.rem(i, 2), z, lax.rem(i, 4) // 2, c)

    bar = pltpu.get_barrier_semaphore()

    def signal(k, carry):
        pl.semaphore_signal(bar, inc=1, device_id=near_dev(lax.rem(near + k, 16)), device_id_type=MESH)
        pl.semaphore_signal(bar, inc=1, device_id=far_dev(lax.rem(far + k, 16)), device_id_type=MESH)
        return carry

    lax.fori_loop(1, 16, signal, 0)
    pl.semaphore_wait(bar, 30)

    def spread(make, stage):
        def step(k, carry):
            make(k).start()
            return carry

        lax.fori_loop(1, 16, step, 0)

    def one(k):
        to = lax.rem(near + k, 16)
        return remote(part.at[to], r1.at[k], ss.at[0], rs.at[0], near_dev(to))

    def two(k):
        to = lax.rem(far + k, 16)
        return remote(s1, r2.at[k], ss.at[1], rs.at[1], far_dev(to))

    def three(k):
        to = lax.rem(near + k, 16)
        return remote(s2, r3.at[k], ss.at[2], rs.at[2], near_dev(to))

    def all_in(ref, stage):
        every = ref.at[pl.ds(1, 15)]
        remote(every, every, ss.at[stage], rs.at[stage], (dp, fs)).wait()

    def ordered(ref, mine):
        def step(i, total):
            return total + ref[lax.rem(mine - i + 16, 16)]

        return lax.fori_loop(0, 16, step, jnp.zeros((24, 128), F32))

    def gin_tile(which, n):
        start = pl.multiple_of(which * DSH, DSH)
        total = jnp.zeros((DSH, 256), F32)
        for g in range(4):
            total += tn(nall[g, :, pl.ds(start, DSH)], pgrad[g, :, pl.ds(n * 256, 256)])
        return total.astype(BF16)

    spread(one, 0)
    for n in range(6):
        give[:, n * 256 : (n + 1) * 256] = gin_tile(fs, n)
    halves = [pl.ds(pl.multiple_of(g * FSH, FSH), FSH) for g in (f, fo)]
    swaps = [
        remote(give.at[:, pl.ds(i * FSH, FSH)], gin.at[:, halves[i]], gs.at[i], gr.at[i], (dp, fs)) for i in range(2)
    ]
    for swap in swaps:
        swap.start()
    r1[0] = part[near]
    all_in(r1, 0)
    s1[...] = ordered(r1, near)
    spread(two, 1)
    for n in range(6):
        base = pl.multiple_of((f if n < 3 else fo) * FSH + (n % 3) * 256, 256)
        gin[:, pl.ds(base, 256)] = gin_tile(f, n)
    r2[0] = s1[...]
    all_in(r2, 1)
    s2[...] = ordered(r2, far)
    spread(three, 2)

    def gout_tile(n, carry):
        w = pl.ds(pl.multiple_of(n * 256, 256), 256)
        total = jnp.zeros((FSH, 256), F32)
        for g in range(4):
            total += tn(hidden[g, :, pl.ds(0, FSH)], masked[g, :, w])
        gout[:, w] = (0.5 * total).astype(BF16)
        return carry

    lax.fori_loop(0, 6, gout_tile, 0)
    r3[0] = s2[...]
    all_in(r3, 2)

    def lay(k, carry):
        ktot[lax.rem(near - k + 16, 16)] = r3[k] * (1.0 / ROWS)
        return carry

    lax.fori_loop(0, 16, lay, 0)
    sib_halves = [pl.ds(pl.multiple_of(g * FSH, FSH), FSH) for g in (fs, (1 - yh) * 2 + 1 - c)]
    for i, swap in enumerate(swaps):
        swap.wait_send()
        got = gin.at[:, sib_halves[i]]
        remote(got, got, gs.at[i], gr.at[i], (dp, fs)).wait_recv()


def last(part, nall, pgrad, hidden, masked):
    slots = pltpu.VMEM((16, 24, 128), F32)
    one = pltpu.VMEM((24, 128), F32)
    return pl.pallas_call(
        last_kernel,
        out_shape=[
            jax.ShapeDtypeStruct((DSH, FF), BF16),
            jax.ShapeDtypeStruct((FSH, D), BF16),
            jax.ShapeDtypeStruct((16, 24, 128), F32),
        ],
        in_specs=[VM] * 5,
        out_specs=[VM] * 3,
        scratch_shapes=[
            slots, one, slots, one, slots,
            pltpu.VMEM((DSH, HALF), BF16),
            pltpu.SemaphoreType.DMA((3,)),
            pltpu.SemaphoreType.DMA((3,)),
            pltpu.SemaphoreType.DMA((2,)),
            pltpu.SemaphoreType.DMA((2,)),
        ],
        compiler_params=pltpu.CompilerParams(collective_id=4, has_side_effects=True, vmem_limit_bytes=VLIM),
        name="last",
    )(part, nall, pgrad, hidden, masked)


def on_device(
    frames, occupied_slot_counts, block_frame_rows, order, cotangent, sub_weight, depth_kernel, norm_gain, w_in, w_out
):
    dp, f, x, yl, z, yh, c = place()
    mine = jnp.concatenate(
        [block_frame_rows[0, 0], occupied_slot_counts[0], jnp.zeros((15,), jnp.int32), order[0]]
    ).reshape(1, 1, 128)
    table = group_table(mine).reshape(4, NDP, 128)
    peers = jnp.arange(NDP, dtype=jnp.int32)
    origin = (dp - peers) % NDP
    counts, ranking = table[:, :, 48], table[:, 0, 64:]
    earlier = origin[:, None] > origin[None, :]
    starts = jnp.sum(jnp.where(earlier[None], counts[:, None, :], 0), axis=2)
    ends = starts + counts
    first = jnp.sum(jnp.where(ranking == dp, peers[None], 0), axis=1)
    wanted = first[:, None] + NDP * jnp.arange(NB, dtype=jnp.int32)[None]
    from_here = (starts[:, None, :] <= wanted[:, :, None]) & (wanted[:, :, None] < ends[:, None, :])
    slot = jnp.sum(jnp.where(from_here, peers, 0), axis=2)
    within = wanted - jnp.sum(jnp.where(from_here, starts[:, None, :], 0), axis=2)
    row_table = jnp.sum(jnp.where(from_here[..., None], table[:, None, :, :NH], 0), axis=2)
    is_slot = within[:, :, None] == jnp.arange(NH, dtype=jnp.int32)
    valid_rows = jnp.sum(jnp.where(is_slot, row_table, 0), axis=2)
    own_rank, own_start = order[0], lax.dynamic_slice(starts, (f, 0), (1, 1))[0, 0]
    residue = jnp.sum(jnp.where(own_rank[None, :] == peers[:, None], peers[None, :], 0), axis=1)
    hsel = jnp.minimum((residue - own_start) % NDP, NH - 1)
    slot_mine = lax.dynamic_index_in_dim(slot, f, 0, keepdims=False)
    relative = jnp.stack([f, (1 - yh) * 2 + c, yh * 2 + 1 - c, (1 - yh) * 2 + 1 - c])
    rel_rows = jnp.sum(
        jnp.where((relative[:, None] == jnp.arange(4))[..., None], valid_rows[None], 0), axis=1
    )
    masks = (
        (jnp.arange(BR, dtype=jnp.int32)[None, :, None] < rel_rows[:, None, :]).astype(F32).reshape(4, ROWS, 1)
    )
    blocks, cots, winh, wouth, suba, _ = move(
        hsel, slot_mine, frames[0, 0], cotangent[0, 0].reshape(ROWS, D), w_in, w_out, sub_weight
    )
    gain = norm_gain.reshape(1, D)
    masked, feat, conv, normed = front(blocks, suba, cots, masks, depth_kernel, gain)
    nall, pgrad, hidden, ngrad = middle(normed, masked, winh, wouth)
    part = tap_terms(ngrad, masked, feat, conv, masks, gain).reshape(16, 24, 128)
    gin, gout, total = last(part, nall, pgrad, hidden, masked)
    return gin[None], gout[None], total.reshape(D // 128, K + 1, 128).transpose(1, 0, 2).reshape(K + 1, D)[:K]


def solution(mesh):
    placed = (
        P("dp", "fsdp", None, None, None),
        P("fsdp", "dp"),
        P("dp", "fsdp", None),
        P("fsdp", None),
        P("dp", "fsdp", None, None, None),
        P("fsdp", None),
        P(),
        P(),
        P("fsdp", None),
        P("fsdp", None),
    )
    return jax.shard_map(
        on_device,
        mesh=mesh,
        in_specs=placed,
        out_specs=(P("dp", "fsdp", None), P("dp", "fsdp", None), P()),
        check_vma=False,
    )
```

time: 660 us -> 278 us (0.42)
  waiting for transfers between devices: 458 us -> 0 us
  Pallas kernels: 0 us -> 257 us
  loops' own time: 41.1 us -> 0 us
  local copies, waits for them, and re-layouts: 48.3 us -> 12.2 us
  matrix products: 35.7 us -> 0 us
  blocking collectives: 22.8 us -> 0 us
  other arithmetic: 22 us -> 6.56 us
  starting transfers between devices: 14.1 us -> 0 us
  between operations: 15.4 us -> 1.42 us
    pallas_call x0 -> x6, Pallas kernels: none -> 257 us  [the longest x1 152 us: move(): pl.pallas_call(move_kernel, out_shape=[jax.ShapeDtypeStruct((2 * NB, 64,...]
    psum x1 -> x0, waiting for transfers between devices: 230 us -> none  [on_device(): kernel_grad = lax.psum(kernel_part, ('dp', 'fsdp')) / row_total]
    reduce_scatter x2 -> x0, waiting for transfers between devices: 184 us -> none  [the longest x1 93.2 us: on_device(): lax.psum_scatter(contract(normed, pre_grad, 0, 0).astype(jnp.bfloat16), '...]
    another operation x1 -> x0, loops' own time: 41.1 us -> none  [prefix(): return lax.fori_loop(0, count - 1, turn, so_far)]
    dynamic_slice x63 -> x1, local copies, waits for them, and re-layouts: 37.3 us -> 0.53 us  [on_device(): lax.dynamic_slice(starts, (f, 0), (1, 1))[0, 0]]
    dot_general x8 -> x0, matrix products: 35.7 us -> none  [the longest x4 24 us: contract(): lax.dot_general(left, right, (((left_dim,), (right_dim,)), ((), ())), pre...]
    all_to_all x3 -> x0, waiting for transfers between devices: 29.5 us -> none  [the longest x1 14.3 us: on_device(): lax.all_to_all(packed, 'dp', split_axis=0, concat_axis=0, tiled=True)]
    unnamed x1 -> x0, blocking collectives: 22.8 us -> none
  transfers between devices with their start and end apart: 9 -> 0, of which waited for: 7 -> 0; matrix products, arithmetic and copies ran while one was open for 12% -> 0% of each run, Pallas kernels for 0% -> 0%
where the time goes in v1:
time: 278 us
  Pallas kernels  257 us (92%)
  local copies, waits for them, and re-layouts  12.2 us (4%)
  other arithmetic  6.56 us (2%)
    pallas_call x1, Pallas kernels, move(): pl.pallas_call(move_kernel, out_shape=[jax.ShapeDtypeStruct((2 * NB, 64,...  152 us
    pallas_call x1, Pallas kernels, last(): pl.pallas_call(last_kernel, out_shape=[jax.ShapeDtypeStruct((DSH, FF), BF...  29.9 us
    pallas_call x1, Pallas kernels, middle(): pl.pallas_call(middle_kernel, out_shape=[jax.ShapeDtypeStruct((4, ROWS, D...  29.2 us
    pallas_call x1, Pallas kernels, group_table(): pl.pallas_call(meta_kernel, out_shape=jax.ShapeDtypeStruct((4 * NDP, 1, 1...  22.9 us
    pallas_call x1, Pallas kernels, front(): pl.pallas_call(front_kernel, out_shape=[jax.ShapeDtypeStruct((4, ROWS, D)...  14.9 us
    pallas_call x1, Pallas kernels, tap_terms(): pl.pallas_call(taps_kernel, out_shape=jax.ShapeDtypeStruct((D // 128, K +...  7.96 us
    unnamed x7, local copies, waits for them, and re-layouts  5.64 us

profile of v1, /device:TPU:1, one launch (start us, length us, event | category | flops | bytes accessed | tf_op | source)
XLA Modules:
  0.0 277.6 jit_solution(15488982580812837400)
XLA Ops:
  1.3 0.1 pad_add_fusion
  1.4 0.1 iota_compare_fusion.2
  1.5 0.8 select_reduce_fusion.5
  2.2 1.3 add_bitcast_fusion.mine
  3.5 1.3 reshape.219.gain
  4.8 0.1 broadcast_compare_fusion
  4.9 0.1 lt.68
  5.0 22.9 %group_table.1 = s32[256,1,128]{2,1,0:T(1,128)} custom-call(s32[1,1,128]{2,1,0:T(1,128)} %add_bitcast_fusion.mine), custom_call_target="tpu_custom_call" | custom-call | tf_op jit(solution)/shard_map/group_table/pallas_call | solution.py:104
  27.9 0.8 slice.21
  28.7 0.1 select_reduce_fusion.7
  28.9 1.0 copy.25
  29.9 1.0 slice.20
  30.9 0.1 copy.29
  31.0 0.2 select_reduce_fusion.1
  31.2 0.5 constant_dynamic-slice_fusion
  31.7 1.2 fusion.hsel
  32.9 0.3 select_reduce_fusion.3
  33.2 1.2 select_reduce_fusion
  34.4 0.2 select_reduce_fusion.2
  34.6 0.1 select_reduce_fusion.6
  34.7 0.5 dynamic-slice_bitcast_fusion.slot
  35.2 0.3 lt.74
  35.5 1.0 compare_convert_fusion.masks
  36.5 152.5 %move.1 = (bf16[32,64,128]{2,1,0:T(8,128)(2,1)}, bf16[4,256,1536]{2,1,0:T(8,128)(2,1)}, bf16[1536,1536]{1,0:T(8,128)(2,1)}, bf16[1536,1536]{1,0:T(8,128)(2,1)}, ...) custom-call(s32[64]{0:T(128)} %fusion.hsel, s32[16]{0:T(128)} %dynamic-slice_bitcast_fusion.slot, ...), custom_call_target="tpu_custom_call" | custom-call | tf_op jit(solution)/shard_map/move/pallas_call | solution.py:275
  189.0 14.9 %front.1 = (bf16[4,256,1536]{2,1,0:T(8,128)(2,1)}, bf16[2,256,1536]{2,1,0:T(8,128)(2,1)}, f32[256,1536]{1,0:T(8,128)}, bf16[2,256,1536]{2,1,0:T(8,128)(2,1)}) custom-call(bf16[32,64,128]{2,1,0:T(8,128)(2,1)} %get-tuple-element.19.blocks, bf16[512,1536]{1,0:T(8,128)(2,1)} %get-tuple-element.20.suba, bf16[4,256,1536]{2,1,0:T(8,128)(2,1)} %get-tuple-element.21.cots, ...), custom_call_target="tpu_custom_call" | custom-call | tf_op jit(solution)/shard_map/front/pallas_call | solution.py:345
  203.9 29.2 %middle.1 = (bf16[4,256,1536]{2,1,0:T(8,128)(2,1)}, bf16[4,256,1536]{2,1,0:T(8,128)(2,1)}, bf16[4,256,1536]{2,1,0:T(8,128)(2,1)}, f32[256,1536]{1,0:T(8,128)}) custom-call(bf16[2,256,1536]{2,1,0:T(8,128)(2,1)} %get-tuple-element.22.normed, bf16[4,256,1536]{2,1,0:T(8,128)(2,1)} %get-tuple-element.23.masked, bf16[1536,1536]{1,0:T(8,128)(2,1)} %get-tuple-element.24.winh, ...), custom_call_target="tpu_custom_call" | custom-call | tf_op jit(solution)/shard_map/middle/pallas_call | solution.py:414
  233.1 8.0 %tap_terms.1 = f32[12,32,128]{2,1,0:T(8,128)} custom-call(f32[256,1536]{1,0:T(8,128)} %get-tuple-element.26.ngrad, bf16[4,256,1536]{2,1,0:T(8,128)(2,1)} %get-tuple-element.23.masked, bf16[2,256,1536]{2,1,0:T(8,128)(2,1)} %get-tuple-element.27.feat, f32[256,1536]{1,0:T(8,128)} %get-tuple-element.28.conv, f32[4,256,1]{2,1,0:T(8,128)} %compare_convert_fusion.masks, ...), custom_call_target="tpu_custom_call" | custom-call | tf_op jit(solution)/shard_map/tap_terms/pallas_call | solution.py:469
  241.0 29.9 %last.1 = (bf16[384,3072]{1,0:T(8,128)(2,1)}, bf16[768,1536]{1,0:T(8,128)(2,1)}, f32[16,24,128]{2,1,0:T(8,128)}) custom-call(f32[16,24,128]{2,1,0:T(8,128)} %bitcast.41, bf16[4,256,1536]{2,1,0:T(8,128)(2,1)} %get-tuple-element.29.nall, bf16[4,256,1536]{2,1,0:T(8,128)(2,1)} %get-tuple-element.30.pgrad, bf16[4,256,1536]{2,1,0:T(8,128)(2,1)} %get-tuple-element.31.hidden, ...), custom_call_target="tpu_custom_call" | custom-call | tf_op jit(solution)/shard_map/last/pallas_call | solution.py:586
  270.9 1.0 copy.33
  272.0 0.7 copy.31
  272.8 3.4 %copy.37 = bf16[1,384,3072]{2,1,0:T(8,128)(2,1)} copy(bf16[1,384,3072]{2,1,0:T(8,128)(2,1)} %bitcast.33) | data formatting | bytes 4718592
  276.2 1.4 copy.38
  (12 shorter events, 0.2 us)
Async XLA Ops:
  272.8 3.4 %copy-start = (bf16[768,1536]{1,0:T(8,128)(2,1)S(1)}, bf16[768,1536]{1,0:T(8,128)(2,1)}, u32[]{:S(2)}) copy-start(bf16[768,1536]{1,0:T(8,128)(2,1)} %get-tuple-element.33) | copy-start | bytes 7077892

commit v2 on v0

v2 whole, which is shorter than its diff:
```python
import functools

import jax
import jax.numpy as jnp
from jax import lax
from jax.experimental import pallas as pl
from jax.experimental.pallas import tpu as pltpu
from jax.sharding import PartitionSpec as P

D = 1536
FF = 3072
K = 31
BR = 16
NB = 16
NH = 48
NDP = 64
ROWS = NB * BR
HALF = FF // 2
FSH = FF // 4
DSH = D // 4
SSH = 128
EPSILON = 1e-05
MESH = pl.DeviceIdType.MESH
F32 = jnp.float32
BF16 = jnp.bfloat16
VLIM = 62 * 1024 * 1024
LANES = 128

ANY = pl.BlockSpec(memory_space=pl.ANY)
VM = pl.BlockSpec(memory_space=pltpu.VMEM)
SM = pl.BlockSpec(memory_space=pltpu.SMEM)


def place():
    dp, f = lax.axis_index("dp"), lax.axis_index("fsdp")
    return dp, f, dp // 16, (dp // 8) % 2, dp % 8, f // 2, f % 2


def dev(x, yl, z, yh, c):
    return ((x * 2 + yl) * 8 + z, yh * 2 + c)


def greet(peers, extra=0):
    bar = pltpu.get_barrier_semaphore()
    for peer in peers:
        pl.semaphore_signal(bar, inc=1, device_id=peer, device_id_type=MESH)
    pl.semaphore_wait(bar, len(peers) + extra)


def remote(src, dst, send, recv, device):
    return pltpu.make_async_remote_copy(
        src_ref=src, dst_ref=dst, send_sem=send, recv_sem=recv, device_id=device, device_id_type=MESH
    )


class Sent:
    def __init__(self, src, dst, ss, rs, i, device):
        self.sems, self.device = (ss.at[i], rs.at[i]), device
        self.copy = remote(src, dst, *self.sems, device)

    def start(self):
        self.copy.start()

    def wait(self):
        self.copy.wait()

    def wait_send(self):
        self.copy.wait_send()

    def wait_got(self, ref):
        remote(ref, ref, *self.sems, self.device).wait_recv()


def nt(left, right):
    return lax.dot_general(left, right, (((1,), (1,)), ((), ())), preferred_element_type=F32)


def tn(left, right):
    return lax.dot_general(left, right, (((0,), (0,)), ((), ())), preferred_element_type=F32)


def lane(start, size):
    return pl.ds(pl.multiple_of(start, LANES), size)


def rows(start, size):
    return pl.ds(pl.multiple_of(start, 16), size)


def kernel(
    inv, mine, frames, taps, gain, cot, w_in, w_out, sub,
    gin, gout, ktot,
    table, stab, ends, sbuf, rbuf, blocks, rowv, cots, masked, winv, woutv, suba, stage,
    hgr, nall, pgrad, hidden, picks, patch, maskv, texp, fch, feat, conv, mix, ngrad, part, got,
    tapp, sums, r1, s1, r2, s2, r3,
    ts, tr, as_, ar, ss, rs, ls, gs, gr,
):
    dp, f, x, yl, z, yh, c = place()
    y = yh * 2 + yl
    fs, fo, fso = yh * 2 + 1 - c, (1 - yh) * 2 + c, (1 - yh) * 2 + 1 - c
    color = lax.rem(x + 2 * z, 4)
    across, mate = dev(x, 1 - yl, z, 1 - yh, c), dev(x, 1 - yl, z, yh, c)
    sibling, other, diagonal = (dp, fs), (dp, fo), (dp, fso)
    xp, xm = dev(lax.rem(x + 1, 4), yl, z, yh, c), dev(lax.rem(x + 3, 4), yl, z, yh, c)
    zp, zm = dev(x, yl, lax.rem(z + 1, 8), yh, c), dev(x, yl, lax.rem(z + 7, 8), yh, c)
    near, far = z * 2 + c, x * 4 + y

    def near_dev(i):
        return dev(x, yl, i // 2, yh, lax.rem(i, 2))

    def far_dev(i):
        return dev(i // 4, lax.rem(i, 2), z, lax.rem(i, 4) // 2, c)

    bar = pltpu.get_barrier_semaphore()

    def signal(k, carry):
        pl.semaphore_signal(bar, inc=1, device_id=(lax.rem(dp + k, NDP), f), device_id_type=MESH)
        return carry

    def signal_near(k, carry):
        pl.semaphore_signal(bar, inc=1, device_id=near_dev(lax.rem(near + k, 16)), device_id_type=MESH)
        pl.semaphore_signal(bar, inc=1, device_id=far_dev(lax.rem(far + k, 16)), device_id_type=MESH)
        return carry

    lax.fori_loop(1, NDP, signal, 0)
    lax.fori_loop(1, 16, signal_near, 0)
    greet([across, sibling, other, diagonal], NDP - 1 + 30)

    count = iter(range(64))

    def rcopy(src, dst, device):
        return Sent(src, dst, ss, rs, next(count), device)

    def cols(g):
        return lane(g * FSH, FSH)

    lo, hi = pl.ds(0, FSH), pl.ds(FSH, FSH)

    table[0] = mine[0]

    def send_table(k, carry):
        remote(mine.at[pl.ds(0, 1)], table.at[pl.ds(k, 1)], ts, tr, (lax.rem(dp + k, NDP), f)).start()
        return carry

    lax.fori_loop(1, NDP, send_table, 0)

    def eighth(size):
        return color * 2 * size + yl * size

    q = rows(eighth(48), 48)
    qd = rows(f * DSH + eighth(48), 48)
    qx = rows(color * 96 + (1 - yl) * 48, 48)
    qxd = rows(f * DSH + color * 96 + (1 - yl) * 48, 48)
    sx = rows(color * 32 + (1 - yl) * 16, 16)
    sxd = rows(f * SSH + color * 32 + (1 - yl) * 16, 16)
    ox = rows(color * 192 + (1 - yl) * 96, 96)
    oxd = rows(FSH + color * 192 + (1 - yl) * 96, 96)
    y_sub = [rcopy(sub.at[sx], suba.at[sxd], across)]
    y_out = [rcopy(w_out.at[ox], woutv.at[oxd], across)]
    y_in = [
        rcopy(w_in.at[qx, cols(fo)], winv.at[qxd, lo], across),
        rcopy(w_in.at[qx, cols(f)], winv.at[qxd, hi], across),
        rcopy(w_in.at[qx, cols(fso)], stage.at[qx, lo], across),
        rcopy(w_in.at[qx, cols(fs)], stage.at[qx, hi], across),
    ]
    for copy in y_sub + y_out + y_in:
        copy.start()
    own = rows(f * DSH, DSH)
    on_chip = [
        rcopy(sub, suba.at[rows(f * SSH, SSH)], sibling),
        rcopy(cot, cots.at[1], sibling),
        rcopy(w_in.at[:, cols(fs)], winv.at[own, lo], sibling),
        rcopy(w_in.at[:, cols(fso)], winv.at[own, hi], sibling),
    ]
    local = [
        pltpu.make_async_copy(cot, cots.at[0], ls.at[0]),
        pltpu.make_async_copy(sub, suba.at[rows(f * SSH, SSH)], ls.at[1]),
        pltpu.make_async_copy(w_out, woutv.at[pl.ds(0, FSH)], ls.at[2]),
        pltpu.make_async_copy(w_in.at[:, cols(f)], winv.at[own, lo], ls.at[3]),
        pltpu.make_async_copy(w_in.at[:, cols(fo)], winv.at[own, hi], ls.at[4]),
    ]
    for copy in on_chip + local:
        copy.start()

    rest = table.at[pl.ds(1, NDP - 1)]
    remote(rest, rest, ts, tr, other).wait()
    to_scalar = pltpu.make_async_copy(table, stab, ls.at[5])
    to_scalar.start()
    to_scalar.wait()

    def running(i, total):
        total = total + stab[lax.rem(dp - i + NDP, NDP), 0, NH]
        ends[i] = total
        return total

    lax.fori_loop(0, NDP, running, 0)
    start = ends[dp] - stab[0, 0, NH]

    def pack(j, carry):
        sbuf[j] = frames[jnp.minimum(lax.rem(inv[j] - start + NDP * NH, NDP), NH - 1)]
        return carry

    lax.fori_loop(0, NDP, pack, 0)

    def send(k, carry):
        to = lax.rem(dp + k, NDP)
        remote(sbuf.at[to], rbuf.at[k], as_, ar, (to, f)).start()
        return carry

    lax.fori_loop(1, NDP, send, 0)
    rbuf[0] = sbuf[dp]

    def to_mate(ref, start, size):
        got_rows = rows(start + eighth(size), size)
        copy = rcopy(ref.at[got_rows], ref.at[got_rows], mate)
        copy.start()
        return copy, ref.at[rows(start + color * 2 * size + (1 - yl) * size, size)]

    def from_mate(pair):
        copy, ref = pair
        copy.wait_send()
        copy.wait_got(ref)

    def forward(ref, start, size):
        a = start + color * size
        full, first, second = rows(a, size), rows(a, size // 2), rows(a + size // 2, size // 2)
        copies = [
            rcopy(ref.at[full], ref.at[full], xp),
            rcopy(ref.at[full], ref.at[full], xm),
            rcopy(ref.at[first], ref.at[first], zp),
            rcopy(ref.at[second], ref.at[second], zm),
        ]
        for copy in copies:
            copy.start()
        left, right = start + lax.rem(color + 3, 4) * size, start + lax.rem(color + 1, 4) * size
        beyond = start + lax.rem(color + 2, 4) * size
        spots = [rows(left, size), rows(right, size), rows(beyond, size // 2), rows(beyond + size // 2, size // 2)]
        return [(copy, ref.at[spot]) for copy, spot in zip(copies, spots)]

    def settle(pairs):
        for copy, ref in pairs:
            copy.wait_send()
        for copy, ref in pairs:
            copy.wait_got(ref)

    y_sub[0].wait_send()
    y_sub[0].wait_got(suba.at[rows(fo * SSH + eighth(16), 16)])
    mate_sub = to_mate(suba, fo * SSH, 16)
    y_out[0].wait_send()
    y_out[0].wait_got(woutv.at[rows(FSH + eighth(96), 96)])
    mate_out = to_mate(woutv, FSH, 96)
    from_mate(mate_sub)
    all_sub = forward(suba, fo * SSH, 32)
    for copy in y_in:
        copy.wait_send()
    qi = rows(fo * DSH + eighth(48), 48)
    for copy, ref in zip(y_in, [winv.at[qi, lo], winv.at[qi, hi], stage.at[q, lo], stage.at[q, hi]]):
        copy.wait_got(ref)
    mate_in, mate_stage = to_mate(winv, fo * DSH, 48), to_mate(stage, 0, 48)
    cot_other = rcopy(cot, cots.at[2], other)
    cot_other.start()
    from_mate(mate_out)
    all_out = forward(woutv, FSH, 192)
    from_mate(mate_in)
    all_in_w = forward(winv, fo * DSH, 96)
    from_mate(mate_stage)
    all_stage = forward(stage, 0, 96)

    r = lax.broadcasted_iota(jnp.int32, (ROWS, 4 * ROWS), 0)
    col = lax.broadcasted_iota(jnp.int32, (ROWS, 4 * ROWS), 1)
    want = lax.rem(r, NB) * (4 * BR) + 4 * (r // NB)
    for k in range(4):
        picks[k] = jnp.where(col == want + k, 1.0, 0.0).astype(BF16)

    def turned(g):
        r = lax.broadcasted_iota(jnp.int32, (ROWS, ROWS), 0)
        col = lax.broadcasted_iota(jnp.int32, (ROWS, ROWS), 1)
        turn = jnp.where(col == lax.rem(r, NB) * BR + r // NB, 1.0, 0.0).astype(BF16)
        return jnp.dot(turn, cots[g], preferred_element_type=F32).astype(BF16)

    def hidden_grads(p):
        span = pl.ds(p * 2 * ROWS, 2 * ROWS)

        def tile(n, carry):
            w = lane(n * 256, 256)
            hgr[span, w] = 0.5 * nt(masked[span, :], woutv[w, :])
            return carry

        lax.fori_loop(0, HALF // 256, tile, 0)

    local[0].wait()
    masked[pl.ds(0, ROWS), :] = turned(0)
    on_chip[1].wait()
    masked[pl.ds(ROWS, ROWS), :] = turned(1)
    settle(all_out)
    local[2].wait()
    hidden_grads(0)

    every = rbuf.at[pl.ds(1, NDP - 1)]
    remote(every, every, as_, ar, other).wait()
    first = inv[dp]

    def select(m, height):
        wanted = first + NDP * m
        at = 0
        for step in (32, 16, 8, 4, 2, 1):
            at = jnp.where(ends[at + step - 1] <= wanted, at + step, at)
        slot = lax.rem(dp - at + NDP, NDP)
        blocks[m] = rbuf[slot]
        within = jnp.clip(wanted - (ends[at] - stab[slot, 0, NH]), 0, NH - 1)
        spot = lax.broadcasted_iota(jnp.int32, (NB, LANES), 0)
        return jnp.where(spot == m, stab[slot, 0, within], height)

    rowv[0] = lax.fori_loop(0, NB, select, jnp.zeros((NB, LANES), jnp.int32))
    here = [
        rcopy(rowv.at[0], rowv.at[1], sibling),
        rcopy(rowv.at[0], rowv.at[2], other),
        rcopy(rowv.at[0], rowv.at[3], diagonal),
        rcopy(blocks.at[pl.ds(0, NB)], blocks.at[pl.ds(NB, NB)], other),
    ]
    for copy in here:
        copy.start()
    settle(all_sub)
    theirs = suba.at[rows(fo * SSH, SSH)]
    sub_sib = rcopy(theirs, theirs, sibling)
    sub_sib.start()
    cot_other.wait()
    cot_sib = rcopy(cots.at[2], cots.at[3], sibling)
    cot_sib.start()
    settle(all_stage)
    stage_sib = rcopy(stage, winv.at[rows(fo * DSH, DSH)], sibling)
    stage_sib.start()
    local[1].wait()
    on_chip[0].wait_send()
    on_chip[0].wait_got(suba.at[rows(fs * SSH, SSH)])
    sub_sib.wait_send()
    sub_sib.wait_got(suba.at[rows(fso * SSH, SSH)])

    def fill_mask(g):
        for t in range(BR):
            maskv[g, pl.ds(t * NB, NB), :] = jnp.where(rowv[g] > t, 1.0, 0.0)

    def front(b, g, row):
        fill_mask(g)
        x_in = blocks[pl.ds(b * NB, NB)].reshape(4 * ROWS, LANES)
        for k in range(4):
            patch[:, pl.ds(k * LANES, LANES)] = jnp.dot(picks[k], x_in, preferred_element_type=F32).astype(BF16)

        def project(n, carry):
            w = lane(n * 256, 256)
            total = jnp.dot(patch[...], suba[:, w], preferred_element_type=F32)
            feat[b, :, w] = (total * maskv[g, :, pl.ds(0, 1)]).astype(BF16)
            return carry

        lax.fori_loop(0, D // 256, project, 0)

        def chunk(l, carry):
            w = lane(l * LANES, LANES)
            for k in range(K):
                texp[pl.ds((K - 1 - k) * NB, NB), :] = jnp.broadcast_to(taps[pl.ds(k, 1), w], (NB, LANES))
            fch[...] = feat[b, :, w].astype(F32)
            total = jnp.zeros((BR, NB, LANES), F32)
            for s in range(BR):
                weights = texp[pl.ds((15 - s) * NB, ROWS), :].reshape(BR, NB, LANES)
                total += weights * fch[pl.ds(s * NB, NB), :][None]
            total = total.reshape(ROWS, LANES)
            if b == 0:
                conv[:, w] = total
            mix[:, w] = fch[...] + maskv[g] * (total * jax.nn.sigmoid(total))
            return carry

        lax.fori_loop(0, D // LANES, chunk, 0)

        def norm(i, carry):
            mixed = mix[rows(i * 64, 64), :]
            mean = jnp.mean(mixed, axis=-1, keepdims=True)
            centred = mixed - mean
            variance = jnp.mean(centred * centred, axis=-1, keepdims=True)
            nall[rows(row + i * 64, 64), :] = (centred * lax.rsqrt(variance + EPSILON) * gain[...]).astype(BF16)
            return carry

        lax.fori_loop(0, ROWS // 64, norm, 0)

    front(0, 0, 0)
    norm_swap = rcopy(nall.at[pl.ds(0, ROWS)], nall.at[pl.ds(ROWS, ROWS)], sibling)
    norm_swap.start()

    settle(all_in_w)
    local[3].wait()
    local[4].wait()
    for i, half in ((2, lo), (3, hi)):
        on_chip[i].wait_send()
        on_chip[i].wait_got(winv.at[rows(fs * DSH, DSH), half])
    stage_sib.wait_send()
    stage_sib.wait_got(winv.at[rows(fso * DSH, DSH)])

    def group(p):
        span = pl.ds(p * 2 * ROWS, 2 * ROWS)

        def tile(n, carry):
            w = lane(n * 256, 256)
            pre = jnp.dot(nall[span, :], winv[:, w], preferred_element_type=F32)
            sig = jax.nn.sigmoid(pre)
            hidden[span, w] = (pre * sig).astype(BF16)
            mask = jnp.concatenate([maskv[2 * p], maskv[2 * p + 1]], axis=0)[:, :1]
            pgrad[span, w] = (mask * hgr[span, w] * (sig * (1.0 + pre * (1.0 - sig)))).astype(BF16)
            return carry

        lax.fori_loop(0, HALF // 256, tile, 0)

    def back(g, ref):
        def tile(n, carry):
            w = lane(n * 256, 256)
            ref[:, w] = nt(pgrad[pl.ds(g * ROWS, ROWS), :], winv[w, :])
            return carry

        lax.fori_loop(0, D // 256, tile, 0)

    here[0].wait()
    fill_mask(1)
    norm_swap.wait()
    group(0)
    back(1, part)
    give = rcopy(part, got, sibling)
    give.start()
    back(0, ngrad)
    give.wait()

    def norm_back(i, carry):
        span = rows(i * 64, 64)
        mask = maskv[0, span, :][:, :1]
        pre = conv[span, :]
        sig = jax.nn.sigmoid(pre)
        mixed = feat[0, span, :].astype(F32) + mask * (pre * sig)
        mean = jnp.mean(mixed, axis=-1, keepdims=True)
        centred = mixed - mean
        scale = lax.rsqrt(jnp.mean(centred * centred, axis=-1, keepdims=True) + EPSILON)
        hat = centred * scale
        dn = (ngrad[span, :] + got[span, :]) * gain[...]
        m1 = jnp.mean(dn, axis=-1, keepdims=True)
        m2 = jnp.mean(dn * hat, axis=-1, keepdims=True)
        total = mask * masked[span, :].astype(F32) + scale * (dn - m1 - hat * m2)
        mix[span, :] = mask * total * (sig * (1.0 + pre * (1.0 - sig)))
        return carry

    lax.fori_loop(0, ROWS // 64, norm_back, 0)

    def tap_chunk(l, carry):
        w = lane(l * LANES, LANES)
        fch[...] = feat[0, :, w].astype(F32)
        for k in range(K):
            t0, t1 = max(0, 15 - k), min(BR, 31 - k)
            size = (t1 - t0) * NB
            term = mix[pl.ds(t0 * NB, size), w] * fch[pl.ds((t0 + k - 15) * NB, size), :]
            sums[pl.ds(k, 1), :] = jnp.sum(term, axis=0, keepdims=True)
        sums[pl.ds(K, 1), :] = jnp.zeros((1, LANES), F32)
        tapp[pl.ds(pl.multiple_of(l * (K + 1), 8), K + 1), :] = sums[...]
        return carry

    lax.fori_loop(0, D // LANES, tap_chunk, 0)

    def spread(make):
        def step(k, carry):
            make(k).start()
            return carry

        lax.fori_loop(1, 16, step, 0)

    def rows24(i):
        return pl.ds(pl.multiple_of(i * 24, 8), 24)

    def one(k):
        to = lax.rem(near + k, 16)
        return remote(tapp.at[rows24(to)], r1.at[k], gs.at[0], gr.at[0], near_dev(to))

    def two(k):
        to = lax.rem(far + k, 16)
        return remote(s1, r2.at[k], gs.at[1], gr.at[1], far_dev(to))

    def three(k):
        to = lax.rem(near + k, 16)
        return remote(s2, r3.at[k], gs.at[2], gr.at[2], near_dev(to))

    def all_here(ref, stage_no):
        every = ref.at[pl.ds(1, 15)]
        remote(every, every, gs.at[stage_no], gr.at[stage_no], sibling).wait()

    def ordered(ref, mine_at):
        def step(i, total):
            return total + ref[lax.rem(mine_at - i + 16, 16)]

        return lax.fori_loop(0, 16, step, jnp.zeros((24, LANES), F32))

    spread(one)
    cot_sib.wait()
    masked[pl.ds(2 * ROWS, ROWS), :] = turned(2)
    masked[pl.ds(3 * ROWS, ROWS), :] = turned(3)
    hidden_grads(1)
    here[1].wait()
    here[3].wait()
    front(1, 2, 2 * ROWS)
    norm_swap2 = rcopy(nall.at[pl.ds(2 * ROWS, ROWS)], nall.at[pl.ds(3 * ROWS, ROWS)], sibling)
    norm_swap2.start()
    here[2].wait()
    fill_mask(3)
    r1[0] = tapp[rows24(near), :]
    all_here(r1, 0)
    s1[...] = ordered(r1, near)
    spread(two)
    for g in range(4):
        if g == 2:
            norm_swap2.wait()
            group(1)
        span = pl.ds(g * ROWS, ROWS)
        masked[span, :] = jnp.where(maskv[g][:, :1] > 0, masked[span, :].astype(F32), 0.0).astype(BF16)
    r2[0] = s1[...]
    all_here(r2, 1)
    s2[...] = ordered(r2, far)
    spread(three)

    def gin_tile(which, n):
        return tn(nall[:, lane(which * DSH, DSH)], pgrad[:, lane(n * 256, 256)]).astype(BF16)

    def give_tile(n, carry):
        stage[:, lane(n * 256, 256)] = gin_tile(fs, n)
        return carry

    lax.fori_loop(0, 6, give_tile, 0)
    swaps = [rcopy(stage.at[:, half], gin.at[:, cols(g)], sibling) for half, g in ((lo, f), (hi, fo))]
    for swap in swaps:
        swap.start()

    def keep_tile(n, carry):
        gin[:, lane(f * FSH + n * 256, 256)] = gin_tile(f, n)
        gin[:, lane(fo * FSH + n * 256, 256)] = gin_tile(f, n + 3)
        return carry

    lax.fori_loop(0, 3, keep_tile, 0)

    def gout_tile(n, carry):
        w = lane(n * 256, 256)
        gout[:, w] = (0.5 * tn(hidden[:, pl.ds(0, FSH)], masked[:, w])).astype(BF16)
        return carry

    lax.fori_loop(0, D // 256, gout_tile, 0)
    r3[0] = s2[...]
    all_here(r3, 2)

    def lay(k, carry):
        ktot[lax.rem(near - k + 16, 16)] = r3[k] * (1.0 / ROWS)
        return carry

    lax.fori_loop(0, 16, lay, 0)
    for swap, g in zip(swaps, (fs, fso)):
        swap.wait_send()
        swap.wait_got(gin.at[:, cols(g)])


def on_device(
    frames, occupied_slot_counts, block_frame_rows, order, cotangent, sub_weight, depth_kernel, norm_gain, w_in, w_out
):
    mine = jnp.concatenate(
        [block_frame_rows[0, 0], occupied_slot_counts[0], jnp.zeros((LANES - NH - 1,), jnp.int32)]
    ).reshape(1, 1, LANES)
    peers = jnp.arange(NDP, dtype=jnp.int32)
    inv = jnp.sum(jnp.where(order[0][None, :] == peers[:, None], peers[None, :], 0), axis=1)
    vm, dma = pltpu.VMEM, pltpu.SemaphoreType.DMA
    slots, one = vm((16, 24, LANES), F32), vm((24, LANES), F32)
    gin, gout, total = pl.pallas_call(
        kernel,
        out_shape=[
            jax.ShapeDtypeStruct((DSH, FF), BF16),
            jax.ShapeDtypeStruct((FSH, D), BF16),
            jax.ShapeDtypeStruct((16, 24, LANES), F32),
        ],
        in_specs=[SM, VM, VM, VM, VM, ANY, ANY, ANY, ANY],
        out_specs=[VM] * 3,
        scratch_shapes=[
            vm((NDP, 1, LANES), jnp.int32),
            pltpu.SMEM((NDP, 1, LANES), jnp.int32),
            pltpu.SMEM((NDP,), jnp.int32),
            vm((NDP, 64, LANES), BF16),
            vm((NDP, 64, LANES), BF16),
            vm((2 * NB, 64, LANES), BF16),
            vm((4, NB, LANES), jnp.int32),
            vm((4, ROWS, D), BF16),
            vm((4 * ROWS, D), BF16),
            vm((D, HALF), BF16),
            vm((HALF, D), BF16),
            vm((4 * SSH, D), BF16),
            vm((DSH, HALF), BF16),
            vm((4 * ROWS, HALF), F32),
            vm((4 * ROWS, D), BF16),
            vm((4 * ROWS, HALF), BF16),
            vm((4 * ROWS, HALF), BF16),
            vm((4, ROWS, 4 * ROWS), BF16),
            vm((ROWS, 4 * LANES), BF16),
            vm((4, ROWS, LANES), F32),
            vm((K * NB, LANES), F32),
            vm((ROWS, LANES), F32),
            vm((2, ROWS, D), BF16),
            vm((ROWS, D), F32),
            vm((ROWS, D), F32),
            vm((ROWS, D), F32),
            vm((ROWS, D), F32),
            vm((ROWS, D), F32),
            vm((D // LANES * (K + 1), LANES), F32),
            vm((K + 1, LANES), F32),
            slots, one, slots, one, slots,
            dma, dma, dma, dma,
            dma((48,)), dma((48,)), dma((6,)), dma((3,)), dma((3,)),
        ],
        compiler_params=pltpu.CompilerParams(collective_id=1, has_side_effects=True, vmem_limit_bytes=VLIM),
        name="window",
    )(
        inv, mine, frames[0, 0], depth_kernel, norm_gain.reshape(1, D),
        cotangent[0, 0].reshape(ROWS, D), w_in, w_out, sub_weight,
    )
    total = total.reshape(D // LANES, K + 1, LANES).transpose(1, 0, 2).reshape(K + 1, D)
    return gin[None], gout[None], total[:K]


def solution(mesh):
    placed = (
        P("dp", "fsdp", None, None, None),
        P("fsdp", "dp"),
        P("dp", "fsdp", None),
        P("fsdp", None),
        P("dp", "fsdp", None, None, None),
        P("fsdp", None),
        P(),
        P(),
        P("fsdp", None),
        P("fsdp", None),
    )
    return jax.shard_map(
        on_device,
        mesh=mesh,
        in_specs=placed,
        out_specs=(P("dp", "fsdp", None), P("dp", "fsdp", None), P()),
        check_vma=False,
    )
```

time: 660 us -> 131 us (0.20)
  waiting for transfers between devices: 458 us -> 0 us
  Pallas kernels: 0 us -> 119 us
  loops' own time: 41.1 us -> 0 us
  local copies, waits for them, and re-layouts: 48.3 us -> 7.9 us
  matrix products: 35.7 us -> 0 us
  blocking collectives: 22.8 us -> 0 us
  other arithmetic: 22 us -> 2.53 us
  starting transfers between devices: 14.1 us -> 0 us
  between operations: 15.4 us -> 1.31 us
    psum x1 -> x0, waiting for transfers between devices: 230 us -> none  [on_device(): kernel_grad = lax.psum(kernel_part, ('dp', 'fsdp')) / row_total]
    reduce_scatter x2 -> x0, waiting for transfers between devices: 184 us -> none  [the longest x1 93.2 us: on_device(): lax.psum_scatter(contract(normed, pre_grad, 0, 0).astype(jnp.bfloat16), '...]
    pallas_call x0 -> x1, Pallas kernels: none -> 119 us  [on_device(): pl.pallas_call(kernel, out_shape=[jax.ShapeDtypeStruct((DSH, FF), BF16),...]
    another operation x1 -> x0, loops' own time: 41.1 us -> none  [prefix(): return lax.fori_loop(0, count - 1, turn, so_far)]
    dynamic_slice x63 -> x0, local copies, waits for them, and re-layouts: 37.3 us -> none  [turn(): longer = join(so_far, pieces[position])]
    dot_general x8 -> x0, matrix products: 35.7 us -> none  [the longest x4 24 us: contract(): lax.dot_general(left, right, (((left_dim,), (right_dim,)), ((), ())), pre...]
    all_to_all x3 -> x0, waiting for transfers between devices: 29.5 us -> none  [the longest x1 14.3 us: on_device(): lax.all_to_all(packed, 'dp', split_axis=0, concat_axis=0, tiled=True)]
    unnamed x1 -> x0, blocking collectives: 22.8 us -> none
  transfers between devices with their start and end apart: 9 -> 0, of which waited for: 7 -> 0; matrix products, arithmetic and copies ran while one was open for 12% -> 0% of each run, Pallas kernels for 0% -> 0%
where the time goes in v2:
time: 131 us; the launch traced here: 130 us
  Pallas kernels  119 us (91%)
  local copies, waits for them, and re-layouts  7.9 us (6%)
  other arithmetic  2.53 us (2%)
  between operations  1.31 us (1%)
    pallas_call x1, Pallas kernels, on_device(): pl.pallas_call(kernel, out_shape=[jax.ShapeDtypeStruct((DSH, FF), BF16),...  119 us
    unnamed x6, local copies, waits for them, and re-layouts  5.54 us

profile of v2, /device:TPU:1, one launch (start us, length us, event | category | flops | bytes accessed | tf_op | source)
XLA Modules:
  0.0 130.4 jit_solution(9455417492326850601)
XLA Ops:
  1.3 1.3 select_reduce_fusion.inv
  2.6 1.2 add_bitcast_fusion.mine
  3.8 1.3 reshape.18.gain
  5.1 118.7 %window.1 = (bf16[384,3072]{1,0:T(8,128)(2,1)}, bf16[768,1536]{1,0:T(8,128)(2,1)}, f32[16,24,128]{2,1,0:T(8,128)}) custom-call(s32[64]{0:T(128)} %select_reduce_fusion.inv, s32[1,1,128]{2,1,0:T(1,128)} %add_bitcast_fusion.mine, bf16[48,64,128]{2,1,0:T(8,128)(2,1)} %bitcast.21, f32[31,1536]{1,0:T(8,128)} %taps.1, f32[1,1536]{1,0:T(1,128)} %reshape.18.gain, ...), custom_call_target="tpu_custom_call" | custom-call | tf_op jit(solution)/shard_map/window/pallas_call | solution.py:569
  123.8 1.0 copy.18
  124.9 0.7 copy.16
  125.6 0.0 copy-start
  125.6 3.4 %copy.22 = bf16[1,384,3072]{2,1,0:T(8,128)(2,1)} copy(bf16[1,384,3072]{2,1,0:T(8,128)(2,1)} %bitcast.18) | data formatting | bytes 4718592
  129.0 0.0 copy-done
  129.0 1.4 %copy.23 = bf16[1,768,1536]{2,1,0:T(8,128)(2,1)} copy(bf16[1,768,1536]{2,1,0:T(8,128)(2,1)S(1)} %bitcast.17) | data formatting | bytes 4718592
  (3 shorter events, 0.0 us)
Async XLA Ops:
  125.6 3.4 %copy-start = (bf16[768,1536]{1,0:T(8,128)(2,1)S(1)}, bf16[768,1536]{1,0:T(8,128)(2,1)}, u32[]{:S(2)}) copy-start(bf16[768,1536]{1,0:T(8,128)(2,1)} %get-tuple-element.7) | copy-start | bytes 7077892

commit v3 on v2

--- a/solution.py
+++ b/solution.py
@@ -88,12 +88,12 @@
 
 
 def kernel(
-    inv, mine, frames, taps, gain, cot, w_in, w_out, sub,
+    count_in, rows_in, order_in, frames_hbm, taps, gain, cot, w_in, w_out, sub,
     gin, gout, ktot,
-    table, stab, ends, sbuf, rbuf, blocks, rowv, cots, masked, winv, woutv, suba, stage,
+    frames, ginv, goutv, mine, invv, inv, slots, table, stab, ends, sbuf, rbuf, blocks, rowv, cots, masked, winv, woutv, suba, stage,
     hgr, nall, pgrad, hidden, picks, patch, maskv, texp, fch, feat, conv, mix, ngrad, part, got,
     tapp, sums, r1, s1, r2, s2, r3,
-    ts, tr, as_, ar, ss, rs, ls, gs, gr,
+    ts, tr, as_, ar, ss, rs, ls, gs, gr, ps, pr, os_,
 ):
     dp, f, x, yl, z, yh, c = place()
     y = yh * 2 + yl
@@ -111,6 +111,10 @@
     def far_dev(i):
         return dev(i // 4, lax.rem(i, 2), z, lax.rem(i, 4) // 2, c)
 
+    frames_in = pltpu.make_async_copy(frames_hbm, frames, ls.at[5])
+    frames_in.start()
+    mine[0] = jnp.full((1, LANES), count_in[0, 0], jnp.int32)
+    mine[0, :, pl.ds(0, NH)] = rows_in[...]
     bar = pltpu.get_barrier_semaphore()
 
     def signal(k, carry):
@@ -118,13 +122,14 @@
         return carry
 
     def signal_near(k, carry):
-        pl.semaphore_signal(bar, inc=1, device_id=near_dev(lax.rem(near + k, 16)), device_id_type=MESH)
-        pl.semaphore_signal(bar, inc=1, device_id=far_dev(lax.rem(far + k, 16)), device_id_type=MESH)
+        zz, xy = lax.rem(z + k, 8), lax.rem(x * 2 + yl + k, 8)
+        pl.semaphore_signal(bar, inc=1, device_id=dev(x, yl, zz, yh, 1 - c), device_id_type=MESH)
+        pl.semaphore_signal(bar, inc=1, device_id=dev(xy // 2, lax.rem(xy, 2), z, 1 - yh, c), device_id_type=MESH)
         return carry
 
     lax.fori_loop(1, NDP, signal, 0)
-    lax.fori_loop(1, 16, signal_near, 0)
-    greet([across, sibling, other, diagonal], NDP - 1 + 30)
+    lax.fori_loop(1, 8, signal_near, 0)
+    greet([sibling, other, diagonal], NDP - 1 + 14)
 
     count = iter(range(64))
 
@@ -143,6 +148,12 @@
         return carry
 
     lax.fori_loop(1, NDP, send_table, 0)
+    home = lax.broadcasted_iota(jnp.int32, (NDP, NDP), 0)
+    residue = lax.broadcasted_iota(jnp.int32, (NDP, NDP), 1)
+    picked = jnp.where(order_in[...] == home, residue, 0)
+    invv[...] = jnp.broadcast_to(jnp.sum(picked, axis=1, keepdims=True), (NDP, LANES))
+    inv_copy = pltpu.make_async_copy(invv, inv, ls.at[6])
+    inv_copy.start()
 
     def eighth(size):
         return color * 2 * size + yl * size
@@ -182,89 +193,94 @@
     for copy in on_chip + local:
         copy.start()
 
-    rest = table.at[pl.ds(1, NDP - 1)]
-    remote(rest, rest, ts, tr, other).wait()
-    to_scalar = pltpu.make_async_copy(table, stab, ls.at[5])
-    to_scalar.start()
-    to_scalar.wait()
-
-    def running(i, total):
-        total = total + stab[lax.rem(dp - i + NDP, NDP), 0, NH]
-        ends[i] = total
-        return total
-
-    lax.fori_loop(0, NDP, running, 0)
-    start = ends[dp] - stab[0, 0, NH]
-
-    def pack(j, carry):
-        sbuf[j] = frames[jnp.minimum(lax.rem(inv[j] - start + NDP * NH, NDP), NH - 1)]
-        return carry
-
-    lax.fori_loop(0, NDP, pack, 0)
-
-    def send(k, carry):
-        to = lax.rem(dp + k, NDP)
-        remote(sbuf.at[to], rbuf.at[k], as_, ar, (to, f)).start()
-        return carry
-
-    lax.fori_loop(1, NDP, send, 0)
-    rbuf[0] = sbuf[dp]
-
-    def to_mate(ref, start, size):
-        got_rows = rows(start + eighth(size), size)
-        copy = rcopy(ref.at[got_rows], ref.at[got_rows], mate)
-        copy.start()
-        return copy, ref.at[rows(start + color * 2 * size + (1 - yl) * size, size)]
-
-    def from_mate(pair):
-        copy, ref = pair
-        copy.wait_send()
-        copy.wait_got(ref)
-
-    def forward(ref, start, size):
-        a = start + color * size
-        full, first, second = rows(a, size), rows(a, size // 2), rows(a + size // 2, size // 2)
-        copies = [
-            rcopy(ref.at[full], ref.at[full], xp),
-            rcopy(ref.at[full], ref.at[full], xm),
-            rcopy(ref.at[first], ref.at[first], zp),
-            rcopy(ref.at[second], ref.at[second], zm),
-        ]
-        for copy in copies:
-            copy.start()
-        left, right = start + lax.rem(color + 3, 4) * size, start + lax.rem(color + 1, 4) * size
-        beyond = start + lax.rem(color + 2, 4) * size
-        spots = [rows(left, size), rows(right, size), rows(beyond, size // 2), rows(beyond + size // 2, size // 2)]
-        return [(copy, ref.at[spot]) for copy, spot in zip(copies, spots)]
-
     def settle(pairs):
         for copy, ref in pairs:
             copy.wait_send()
         for copy, ref in pairs:
             copy.wait_got(ref)
 
+    def eighths(start, size, shift, part_of):
+        return rows(start + lax.rem(color + shift, 4) * 2 * size + part_of * size, size)
+
+    def pass_on(ref, start, size):
+        here = ref.at[eighths(start, size, 0, yl)]
+        copies = [rcopy(here, here, peer) for peer in (mate, xp, xm, zp)]
+        for copy in copies:
+            copy.start()
+        spots = [(0, 1 - yl), (3, yl), (1, yl), (2, yl)]
+        return [(copy, ref.at[eighths(start, size, *spot)]) for copy, spot in zip(copies, spots)]
+
+    def pass_mate(ref, start, size, pairs):
+        settle(pairs[:1])
+        here = ref.at[eighths(start, size, 0, 1 - yl)]
+        copies = [rcopy(here, here, peer) for peer in (xp, xm, zm)]
+        for copy in copies:
+            copy.start()
+        spots = [(3, 1 - yl), (1, 1 - yl), (2, 1 - yl)]
+        return pairs[1:] + [(copy, ref.at[eighths(start, size, *spot)]) for copy, spot in zip(copies, spots)]
+
     y_sub[0].wait_send()
     y_sub[0].wait_got(suba.at[rows(fo * SSH + eighth(16), 16)])
-    mate_sub = to_mate(suba, fo * SSH, 16)
+    all_sub = pass_on(suba, fo * SSH, 16)
+
+    rest = table.at[pl.ds(1, NDP - 1)]
+    remote(rest, rest, ts, tr, other).wait()
+    to_scalar = pltpu.make_async_copy(table, stab, ls.at[7])
+    to_scalar.start()
+    to_scalar.wait()
+    inv_copy.wait()
+    frames_in.wait()
+
+    def running(i, total):
+        total = total + stab[lax.rem(dp - i + NDP, NDP), 0, NH]
+        ends[i] = total
+        return total
+
+    lax.fori_loop(0, NDP, running, 0)
+    start = ends[dp] - stab[0, 0, NH]
+
+    def pick_home(j):
+        return frames[jnp.minimum(lax.rem(inv[j, 0] - start + NDP * NH, NDP), NH - 1)]
+
+    def send(k, carry):
+        kk = lax.rem(k * 27, NDP)
+        to = lax.rem(dp + kk, NDP)
+        sbuf[to] = pick_home(to)
+        remote(sbuf.at[to], rbuf.at[kk], as_, ar, (to, f)).start()
+        return carry
+
+    lax.fori_loop(1, NDP, send, 0)
+    rbuf[0] = pick_home(dp)
+
     y_out[0].wait_send()
     y_out[0].wait_got(woutv.at[rows(FSH + eighth(96), 96)])
-    mate_out = to_mate(woutv, FSH, 96)
-    from_mate(mate_sub)
-    all_sub = forward(suba, fo * SSH, 32)
+    all_out = pass_on(woutv, FSH, 96)
+    all_sub = pass_mate(suba, fo * SSH, 16, all_sub)
     for copy in y_in:
         copy.wait_send()
     qi = rows(fo * DSH + eighth(48), 48)
     for copy, ref in zip(y_in, [winv.at[qi, lo], winv.at[qi, hi], stage.at[q, lo], stage.at[q, hi]]):
         copy.wait_got(ref)
-    mate_in, mate_stage = to_mate(winv, fo * DSH, 48), to_mate(stage, 0, 48)
-    cot_other = rcopy(cot, cots.at[2], other)
-    cot_other.start()
-    from_mate(mate_out)
-    all_out = forward(woutv, FSH, 192)
-    from_mate(mate_in)
-    all_in_w = forward(winv, fo * DSH, 96)
-    from_mate(mate_stage)
-    all_stage = forward(stage, 0, 96)
+    all_stage = pass_on(stage, 0, 48)
+    all_in_w = pass_on(winv, fo * DSH, 48)
+    all_out = pass_mate(woutv, FSH, 96, all_out)
+    all_stage = pass_mate(stage, 0, 48, all_stage)
+    all_in_w = pass_mate(winv, fo * DSH, 48, all_in_w)
+
+    first = inv[dp, 0]
+
+    def choose(m, height):
+        wanted = first + NDP * m
+        at = 0
+        for step in (32, 16, 8, 4, 2, 1):
+            at = jnp.where(ends[at + step - 1] <= wanted, at + step, at)
+        slot = lax.rem(dp - at + NDP, NDP)
+        within = jnp.clip(wanted - (ends[at] - stab[slot, 0, NH]), 0, NH - 1)
+        slots[m] = slot
+        spot = lax.broadcasted_iota(jnp.int32, (NB, LANES), 0)
+        return jnp.where(spot == m, stab[slot, 0, within], height)
+
+    rowv[0] = lax.fori_loop(0, NB, choose, jnp.zeros((NB, LANES), jnp.int32))
 
     r = lax.broadcasted_iota(jnp.int32, (ROWS, 4 * ROWS), 0)
     col = lax.broadcasted_iota(jnp.int32, (ROWS, 4 * ROWS), 1)
@@ -292,26 +308,15 @@
     masked[pl.ds(0, ROWS), :] = turned(0)
     on_chip[1].wait()
     masked[pl.ds(ROWS, ROWS), :] = turned(1)
-    settle(all_out)
-    local[2].wait()
-    hidden_grads(0)
 
     every = rbuf.at[pl.ds(1, NDP - 1)]
     remote(every, every, as_, ar, other).wait()
-    first = inv[dp]
-
-    def select(m, height):
-        wanted = first + NDP * m
-        at = 0
-        for step in (32, 16, 8, 4, 2, 1):
-            at = jnp.where(ends[at + step - 1] <= wanted, at + step, at)
-        slot = lax.rem(dp - at + NDP, NDP)
-        blocks[m] = rbuf[slot]
-        within = jnp.clip(wanted - (ends[at] - stab[slot, 0, NH]), 0, NH - 1)
-        spot = lax.broadcasted_iota(jnp.int32, (NB, LANES), 0)
-        return jnp.where(spot == m, stab[slot, 0, within], height)
-
-    rowv[0] = lax.fori_loop(0, NB, select, jnp.zeros((NB, LANES), jnp.int32))
+
+    def select(m, carry):
+        blocks[m] = rbuf[slots[m]]
+        return carry
+
+    lax.fori_loop(0, NB, select, 0)
     here = [
         rcopy(rowv.at[0], rowv.at[1], sibling),
         rcopy(rowv.at[0], rowv.at[2], other),
@@ -320,13 +325,12 @@
     ]
     for copy in here:
         copy.start()
+    cot_other = rcopy(cot, cots.at[2], other)
+    cot_other.start()
     settle(all_sub)
     theirs = suba.at[rows(fo * SSH, SSH)]
     sub_sib = rcopy(theirs, theirs, sibling)
     sub_sib.start()
-    cot_other.wait()
-    cot_sib = rcopy(cots.at[2], cots.at[3], sibling)
-    cot_sib.start()
     settle(all_stage)
     stage_sib = rcopy(stage, winv.at[rows(fo * DSH, DSH)], sibling)
     stage_sib.start()
@@ -376,14 +380,25 @@
             mean = jnp.mean(mixed, axis=-1, keepdims=True)
             centred = mixed - mean
             variance = jnp.mean(centred * centred, axis=-1, keepdims=True)
-            nall[rows(row + i * 64, 64), :] = (centred * lax.rsqrt(variance + EPSILON) * gain[...]).astype(BF16)
+            nall[rows(row + i * 64, 64), :] = (centred * lax.rsqrt(variance + EPSILON) * gain[...][None, :]).astype(BF16)
+            swap = nall.at[rows(row + i * 64, 64)], nall.at[rows(row + ROWS + i * 64, 64)]
+            remote(*swap, ps.at[b * 4 + i], pr.at[b * 4 + i], sibling).start()
             return carry
 
         lax.fori_loop(0, ROWS // 64, norm, 0)
 
+    def norm_here(b, row):
+        def step(i, carry):
+            swap = nall.at[rows(row + i * 64, 64)], nall.at[rows(row + ROWS + i * 64, 64)]
+            remote(*swap, ps.at[b * 4 + i], pr.at[b * 4 + i], sibling).wait()
+            return carry
+
+        lax.fori_loop(0, ROWS // 64, step, 0)
+
     front(0, 0, 0)
-    norm_swap = rcopy(nall.at[pl.ds(0, ROWS)], nall.at[pl.ds(ROWS, ROWS)], sibling)
-    norm_swap.start()
+    settle(all_out)
+    local[2].wait()
+    hidden_grads(0)
 
     settle(all_in_w)
     local[3].wait()
@@ -408,23 +423,32 @@
 
         lax.fori_loop(0, HALF // 256, tile, 0)
 
+    def given(n):
+        w = lane(n * 256, 256)
+        return remote(part.at[:, w], got.at[:, w], ps.at[8 + n], pr.at[8 + n], sibling)
+
     def back(g, ref):
         def tile(n, carry):
             w = lane(n * 256, 256)
             ref[:, w] = nt(pgrad[pl.ds(g * ROWS, ROWS), :], winv[w, :])
+            if g == 1:
+                given(n).start()
             return carry
 
         lax.fori_loop(0, D // 256, tile, 0)
 
     here[0].wait()
     fill_mask(1)
-    norm_swap.wait()
+    norm_here(0, 0)
     group(0)
     back(1, part)
-    give = rcopy(part, got, sibling)
-    give.start()
     back(0, ngrad)
-    give.wait()
+
+    def take(n, carry):
+        given(n).wait()
+        return carry
+
+    lax.fori_loop(0, D // 256, take, 0)
 
     def norm_back(i, carry):
         span = rows(i * 64, 64)
@@ -436,7 +460,7 @@
         centred = mixed - mean
         scale = lax.rsqrt(jnp.mean(centred * centred, axis=-1, keepdims=True) + EPSILON)
         hat = centred * scale
-        dn = (ngrad[span, :] + got[span, :]) * gain[...]
+        dn = (ngrad[span, :] + got[span, :]) * gain[...][None, :]
         m1 = jnp.mean(dn, axis=-1, keepdims=True)
         m2 = jnp.mean(dn * hat, axis=-1, keepdims=True)
         total = mask * masked[span, :].astype(F32) + scale * (dn - m1 - hat * m2)
@@ -492,24 +516,25 @@
         return lax.fori_loop(0, 16, step, jnp.zeros((24, LANES), F32))
 
     spread(one)
-    cot_sib.wait()
-    masked[pl.ds(2 * ROWS, ROWS), :] = turned(2)
-    masked[pl.ds(3 * ROWS, ROWS), :] = turned(3)
-    hidden_grads(1)
     here[1].wait()
     here[3].wait()
     front(1, 2, 2 * ROWS)
-    norm_swap2 = rcopy(nall.at[pl.ds(2 * ROWS, ROWS)], nall.at[pl.ds(3 * ROWS, ROWS)], sibling)
-    norm_swap2.start()
     here[2].wait()
     fill_mask(3)
     r1[0] = tapp[rows24(near), :]
     all_here(r1, 0)
     s1[...] = ordered(r1, near)
     spread(two)
+    cot_other.wait()
+    cot_sib = rcopy(cots.at[2], cots.at[3], sibling)
+    cot_sib.start()
+    masked[pl.ds(2 * ROWS, ROWS), :] = turned(2)
+    cot_sib.wait()
+    masked[pl.ds(3 * ROWS, ROWS), :] = turned(3)
+    hidden_grads(1)
     for g in range(4):
         if g == 2:
-            norm_swap2.wait()
+            norm_here(1, 2 * ROWS)
             group(1)
         span = pl.ds(g * ROWS, ROWS)
         masked[span, :] = jnp.where(maskv[g][:, :1] > 0, masked[span, :].astype(F32), 0.0).astype(BF16)
@@ -526,56 +551,79 @@
         return carry
 
     lax.fori_loop(0, 6, give_tile, 0)
-    swaps = [rcopy(stage.at[:, half], gin.at[:, cols(g)], sibling) for half, g in ((lo, f), (hi, fo))]
+    swaps = [rcopy(stage.at[:, half], ginv.at[:, cols(g)], sibling) for half, g in ((lo, f), (hi, fo))]
     for swap in swaps:
         swap.start()
 
+    def leave(ref, out, w, i):
+        return pltpu.make_async_copy(ref.at[:, w], out.at[:, w], os_.at[i])
+
     def keep_tile(n, carry):
-        gin[:, lane(f * FSH + n * 256, 256)] = gin_tile(f, n)
-        gin[:, lane(fo * FSH + n * 256, 256)] = gin_tile(f, n + 3)
+        first, second = lane(f * FSH + n * 256, 256), lane(fo * FSH + n * 256, 256)
+        ginv[:, first] = gin_tile(f, n)
+        leave(ginv, gin, first, n).start()
+        ginv[:, second] = gin_tile(f, n + 3)
+        leave(ginv, gin, second, 3 + n).start()
         return carry
 
     lax.fori_loop(0, 3, keep_tile, 0)
 
     def gout_tile(n, carry):
         w = lane(n * 256, 256)
-        gout[:, w] = (0.5 * tn(hidden[:, pl.ds(0, FSH)], masked[:, w])).astype(BF16)
+        goutv[:, w] = (0.5 * tn(hidden[:, pl.ds(0, FSH)], masked[:, w])).astype(BF16)
+        leave(goutv, gout, w, 6 + n).start()
         return carry
 
     lax.fori_loop(0, D // 256, gout_tile, 0)
+    for i, (swap, g) in enumerate(zip(swaps, (fs, fso))):
+        swap.wait_send()
+        swap.wait_got(ginv.at[:, cols(g)])
+        leave(ginv, gin, cols(g), 12 + i).start()
     r3[0] = s2[...]
     all_here(r3, 2)
 
     def lay(k, carry):
-        ktot[lax.rem(near - k + 16, 16)] = r3[k] * (1.0 / ROWS)
+        tapp[rows24(lax.rem(near - k + 16, 16)), :] = r3[k] * (1.0 / ROWS)
         return carry
 
     lax.fori_loop(0, 16, lay, 0)
-    for swap, g in zip(swaps, (fs, fso)):
-        swap.wait_send()
-        swap.wait_got(gin.at[:, cols(g)])
+    for l in range(D // LANES):
+        ktot[:, pl.ds(l * LANES, LANES)] = tapp[pl.ds(l * (K + 1), K), :]
+
+    def gone(n, carry):
+        leave(ginv, gin, lane(f * FSH + n * 256, 256), n).wait()
+        leave(ginv, gin, lane(fo * FSH + n * 256, 256), 3 + n).wait()
+        leave(goutv, gout, lane(n * 256, 256), 6 + n).wait()
+        leave(goutv, gout, lane((n + 3) * 256, 256), 9 + n).wait()
+        return carry
+
+    lax.fori_loop(0, 3, gone, 0)
+    for i, g in enumerate((fs, fso)):
+        leave(ginv, gin, cols(g), 12 + i).wait()
 
 
 def on_device(
     frames, occupied_slot_counts, block_frame_rows, order, cotangent, sub_weight, depth_kernel, norm_gain, w_in, w_out
 ):
-    mine = jnp.concatenate(
-        [block_frame_rows[0, 0], occupied_slot_counts[0], jnp.zeros((LANES - NH - 1,), jnp.int32)]
-    ).reshape(1, 1, LANES)
-    peers = jnp.arange(NDP, dtype=jnp.int32)
-    inv = jnp.sum(jnp.where(order[0][None, :] == peers[:, None], peers[None, :], 0), axis=1)
     vm, dma = pltpu.VMEM, pltpu.SemaphoreType.DMA
-    slots, one = vm((16, 24, LANES), F32), vm((24, LANES), F32)
+    stages, one = vm((16, 24, LANES), F32), vm((24, LANES), F32)
     gin, gout, total = pl.pallas_call(
         kernel,
         out_shape=[
             jax.ShapeDtypeStruct((DSH, FF), BF16),
             jax.ShapeDtypeStruct((FSH, D), BF16),
-            jax.ShapeDtypeStruct((16, 24, LANES), F32),
+            jax.ShapeDtypeStruct((K, D), F32),
         ],
-        in_specs=[SM, VM, VM, VM, VM, ANY, ANY, ANY, ANY],
-        out_specs=[VM] * 3,
+        in_specs=[SM, VM, VM, ANY, VM, VM, ANY, ANY, ANY, ANY],
+        out_specs=[ANY, ANY, VM],
         scratch_shapes=[
+            vm((NH, 64, LANES), BF16),
+            vm((DSH, FF), BF16),
+            vm((FSH, D), BF16),
+            vm((1, 1, LANES), jnp.int32),
+            vm((NDP, LANES), jnp.int32),
+            pltpu.SMEM((NDP, LANES), jnp.int32),
+            pltpu.SMEM((NB,), jnp.int32),
             vm((NDP, 1, LANES), jnp.int32),
             pltpu.SMEM((NDP, 1, LANES), jnp.int32),
             pltpu.SMEM((NDP,), jnp.int32),
@@ -606,18 +654,17 @@
             vm((ROWS, D), F32),
             vm((D // LANES * (K + 1), LANES), F32),
             vm((K + 1, LANES), F32),
-            slots, one, slots, one, slots,
+            stages, one, stages, one, stages,
             dma, dma, dma, dma,
-            dma((48,)), dma((48,)), dma((6,)), dma((3,)), dma((3,)),
+            dma((56,)), dma((56,)), dma((8,)), dma((3,)), dma((3,)), dma((14,)), dma((14,)), dma((14,)),
         ],
         compiler_params=pltpu.CompilerParams(collective_id=1, has_side_effects=True, vmem_limit_bytes=VLIM),
         name="window",
     )(
-        inv, mine, frames[0, 0], depth_kernel, norm_gain.reshape(1, D),
+        occupied_slot_counts, block_frame_rows[0], order, frames[0, 0], depth_kernel, norm_gain,
         cotangent[0, 0].reshape(ROWS, D), w_in, w_out, sub_weight,
     )
-    total = total.reshape(D // LANES, K + 1, LANES).transpose(1, 0, 2).reshape(K + 1, D)
-    return gin[None], gout[None], total[:K]
+    return gin[None], gout[None], total
 
 
 def solution(mesh):

time: 131 us -> 118 us (0.901)
  Pallas kernels: 119 us -> 111 us
  other arithmetic: 2.53 us -> 0 us
  local copies, waits for them, and re-layouts: 7.9 us -> 5.46 us
    pallas_call x1, Pallas kernels: 119 us -> 111 us  [on_device(): pl.pallas_call(kernel, out_shape=[jax.ShapeDtypeStruct((DSH, FF), BF16),...]
    reshape x2 -> x0, local copies, waits for them, and re-layouts: 2.34 us -> none  [the longest x1 1.29 us: on_device(): norm_gain.reshape(1, D)]
    unnamed x6 -> x7, local copies, waits for them, and re-layouts: 5.54 us -> 5.46 us
where the time goes in v3:
time: 118 us
  Pallas kernels  111 us (94%)
  local copies, waits for them, and re-layouts  5.46 us (5%)
  between operations  1.3 us (1%)
    pallas_call x1, Pallas kernels, on_device(): pl.pallas_call(kernel, out_shape=[jax.ShapeDtypeStruct((DSH, FF), BF16),...  111 us
    unnamed x7, local copies, waits for them, and re-layouts  5.46 us

profile of v3, /device:TPU:1, one launch (start us, length us, event | category | flops | bytes accessed | tf_op | source)
XLA Modules:
  0.0 118.0 jit_solution(3867383790362792066)
XLA Ops:
  1.3 111.2 %window.1 = (bf16[384,3072]{1,0:T(8,128)(2,1)}, bf16[768,1536]{1,0:T(8,128)(2,1)}, f32[31,1536]{1,0:T(8,128)}) custom-call(s32[1,1]{1,0:T(1,128)S(6)} %copy.16.count_in, s32[1,48]{1,0:T(1,128)} %bitcast.9, s32[1,64]{1,0:T(1,128)} %order_in.1, bf16[48,64,128]{2,1,0:T(8,128)(2,1)} %bitcast.7, f32[31,1536]{1,0:T(8,128)} %taps.1, f32[1536]{0:T(1024)} %gain.1, ...), custom_call_target="tpu_custom_call" | custom-call | tf_op jit(solution)/shard_map/window/pallas_call | solution.py:610
  112.5 0.0 copy-start
  112.5 3.4 %copy.17 = bf16[1,384,3072]{2,1,0:T(8,128)(2,1)} copy(bf16[1,384,3072]{2,1,0:T(8,128)(2,1)} %bitcast.6) | data formatting | bytes 4718592
  115.9 0.0 copy-done
  115.9 0.0 copy-start.1
  115.9 1.4 %copy.18 = bf16[1,768,1536]{2,1,0:T(8,128)(2,1)} copy(bf16[1,768,1536]{2,1,0:T(8,128)(2,1)S(1)} %bitcast.5) | data formatting | bytes 4718592
  117.3 0.0 copy-done.1
  117.3 0.7 copy.19
Async XLA Ops:
  112.5 3.4 %copy-start = (bf16[768,1536]{1,0:T(8,128)(2,1)S(1)}, bf16[768,1536]{1,0:T(8,128)(2,1)}, u32[]{:S(2)}) copy-start(bf16[768,1536]{1,0:T(8,128)(2,1)} %get-tuple-element.7) | copy-start | bytes 7077892
  115.9 1.4 %copy-start.1 = (f32[31,1536]{1,0:T(8,128)S(1)}, f32[31,1536]{1,0:T(8,128)}, u32[]{:S(2)}) copy-start(f32[31,1536]{1,0:T(8,128)} %get-tuple-element.14) | copy-start | bytes 571396

commit v4 on v3

--- a/solution.py
+++ b/solution.py
@@ -75,10 +75,6 @@
     return lax.dot_general(left, right, (((1,), (1,)), ((), ())), preferred_element_type=F32)
 
 
-def tn(left, right):
-    return lax.dot_general(left, right, (((0,), (0,)), ((), ())), preferred_element_type=F32)
-
-
 def lane(start, size):
     return pl.ds(pl.multiple_of(start, LANES), size)
 
@@ -91,7 +87,7 @@
     count_in, rows_in, order_in, frames_hbm, taps, gain, cot, w_in, w_out, sub,
     gin, gout, ktot,
     frames, ginv, goutv, mine, invv, inv, slots, table, stab, ends, sbuf, rbuf, blocks, rowv, cots, masked, winv, woutv, suba, stage,
-    hgr, nall, pgrad, hidden, picks, patch, maskv, texp, fch, feat, conv, mix, ngrad, part, got,
+    hgr, nall, pgrad, hturn, nturn, picks, patch, maskv, texp, fch, feat, conv, mix, ngrad, part, got,
     tapp, sums, r1, s1, r2, s2, r3,
     ts, tr, as_, ar, ss, rs, ls, gs, gr, ps, pr, os_,
 ):
@@ -309,6 +305,11 @@
     on_chip[1].wait()
     masked[pl.ds(ROWS, ROWS), :] = turned(1)
 
+    settle(all_sub)
+    theirs = suba.at[rows(fo * SSH, SSH)]
+    sub_sib = rcopy(theirs, theirs, sibling)
+    sub_sib.start()
+
     every = rbuf.at[pl.ds(1, NDP - 1)]
     remote(every, every, as_, ar, other).wait()
 
@@ -327,13 +328,6 @@
         copy.start()
     cot_other = rcopy(cot, cots.at[2], other)
     cot_other.start()
-    settle(all_sub)
-    theirs = suba.at[rows(fo * SSH, SSH)]
-    sub_sib = rcopy(theirs, theirs, sibling)
-    sub_sib.start()
-    settle(all_stage)
-    stage_sib = rcopy(stage, winv.at[rows(fo * DSH, DSH)], sibling)
-    stage_sib.start()
     local[1].wait()
     on_chip[0].wait_send()
     on_chip[0].wait_got(suba.at[rows(fs * SSH, SSH)])
@@ -396,10 +390,55 @@
         lax.fori_loop(0, ROWS // 64, step, 0)
 
     front(0, 0, 0)
+    settle(all_stage)
+    stage_sib = rcopy(stage, winv.at[rows(fo * DSH, DSH)], sibling)
+    stage_sib.start()
     settle(all_out)
     local[2].wait()
     hidden_grads(0)
 
+    def group(p):
+        span = pl.ds(p * 2 * ROWS, 2 * ROWS)
+
+        def tile(n, with_hidden):
+            w = lane(n * 256, 256)
+            pre = jnp.dot(nall[span, :], winv[:, w], preferred_element_type=F32)
+            sig = jax.nn.sigmoid(pre)
+            if with_hidden:
+                hturn[rows(n * 256, 256), span] = (pre * sig).astype(BF16).T
+            mask = jnp.concatenate([maskv[2 * p], maskv[2 * p + 1]], axis=0)[:, :1]
+            pgrad[span, w] = (mask * hgr[span, w] * (sig * (1.0 + pre * (1.0 - sig)))).astype(BF16)
+
+        def both(n, carry):
+            tile(n, True)
+            tile(n + 3, False)
+            return carry
+
+        lax.fori_loop(0, HALF // 512, both, 0)
+
+    def turn_normed(p):
+        span = pl.ds(p * 2 * ROWS, 2 * ROWS)
+        for i, which in enumerate((fs, f)):
+            nturn[pl.ds(i * DSH, DSH), span] = nall[span, lane(which * DSH, DSH)].T
+
+    def given(n):
+        w = lane(n * 256, 256)
+        return remote(part.at[:, w], got.at[:, w], ps.at[8 + n], pr.at[8 + n], sibling)
+
+    def back(g, ref):
+        def tile(n, carry):
+            w = lane(n * 256, 256)
+            ref[:, w] = nt(pgrad[pl.ds(g * ROWS, ROWS), :], winv[w, :])
+            if g == 1:
+                given(n).start()
+            return carry
+
+        lax.fori_loop(0, D // 256, tile, 0)
+
+    here[0].wait()
+    fill_mask(1)
+    norm_here(0, 0)
+    turn_normed(0)
     settle(all_in_w)
     local[3].wait()
     local[4].wait()
@@ -408,38 +447,6 @@
         on_chip[i].wait_got(winv.at[rows(fs * DSH, DSH), half])
     stage_sib.wait_send()
     stage_sib.wait_got(winv.at[rows(fso * DSH, DSH)])
-
-    def group(p):
-        span = pl.ds(p * 2 * ROWS, 2 * ROWS)
-
-        def tile(n, carry):
-            w = lane(n * 256, 256)
-            pre = jnp.dot(nall[span, :], winv[:, w], preferred_element_type=F32)
-            sig = jax.nn.sigmoid(pre)
-            hidden[span, w] = (pre * sig).astype(BF16)
-            mask = jnp.concatenate([maskv[2 * p], maskv[2 * p + 1]], axis=0)[:, :1]
-            pgrad[span, w] = (mask * hgr[span, w] * (sig * (1.0 + pre * (1.0 - sig)))).astype(BF16)
-            return carry
-
-        lax.fori_loop(0, HALF // 256, tile, 0)
-
-    def given(n):
-        w = lane(n * 256, 256)
-        return remote(part.at[:, w], got.at[:, w], ps.at[8 + n], pr.at[8 + n], sibling)
-
-    def back(g, ref):
-        def tile(n, carry):
-            w = lane(n * 256, 256)
-            ref[:, w] = nt(pgrad[pl.ds(g * ROWS, ROWS), :], winv[w, :])
-            if g == 1:
-                given(n).start()
-            return carry
-
-        lax.fori_loop(0, D // 256, tile, 0)
-
-    here[0].wait()
-    fill_mask(1)
-    norm_here(0, 0)
     group(0)
     back(1, part)
     back(0, ngrad)
@@ -535,6 +542,7 @@
     for g in range(4):
         if g == 2:
             norm_here(1, 2 * ROWS)
+            turn_normed(1)
             group(1)
         span = pl.ds(g * ROWS, ROWS)
         masked[span, :] = jnp.where(maskv[g][:, :1] > 0, masked[span, :].astype(F32), 0.0).astype(BF16)
@@ -543,11 +551,13 @@
     s2[...] = ordered(r2, far)
     spread(three)
 
-    def gin_tile(which, n):
-        return tn(nall[:, lane(which * DSH, DSH)], pgrad[:, lane(n * 256, 256)]).astype(BF16)
+    def gin_tile(i, n):
+        return jnp.dot(
+            nturn[pl.ds(i * DSH, DSH), :], pgrad[:, lane(n * 256, 256)], preferred_element_type=F32
+        ).astype(BF16)
 
     def give_tile(n, carry):
-        stage[:, lane(n * 256, 256)] = gin_tile(fs, n)
+        stage[:, lane(n * 256, 256)] = gin_tile(0, n)
         return carry
 
     lax.fori_loop(0, 6, give_tile, 0)
@@ -560,9 +570,9 @@
 
     def keep_tile(n, carry):
         first, second = lane(f * FSH + n * 256, 256), lane(fo * FSH + n * 256, 256)
-        ginv[:, first] = gin_tile(f, n)
+        ginv[:, first] = gin_tile(1, n)
         leave(ginv, gin, first, n).start()
-        ginv[:, second] = gin_tile(f, n + 3)
+        ginv[:, second] = gin_tile(1, n + 3)
         leave(ginv, gin, second, 3 + n).start()
         return carry
 
@@ -570,7 +580,7 @@
 
     def gout_tile(n, carry):
         w = lane(n * 256, 256)
-        goutv[:, w] = (0.5 * tn(hidden[:, pl.ds(0, FSH)], masked[:, w])).astype(BF16)
+        goutv[:, w] = (0.5 * jnp.dot(hturn[...], masked[:, w], preferred_element_type=F32)).astype(BF16)
         leave(goutv, gout, w, 6 + n).start()
         return carry
 
@@ -640,7 +650,8 @@
             vm((4 * ROWS, HALF), F32),
             vm((4 * ROWS, D), BF16),
             vm((4 * ROWS, HALF), BF16),
-            vm((4 * ROWS, HALF), BF16),
+            vm((FSH, 4 * ROWS), BF16),
+            vm((2 * DSH, 4 * ROWS), BF16),
             vm((4, ROWS, 4 * ROWS), BF16),
             vm((ROWS, 4 * LANES), BF16),
             vm((4, ROWS, LANES), F32),

time: 118 us -> 112 us (0.949)
  Pallas kernels: 111 us -> 105 us
    pallas_call x1, Pallas kernels: 111 us -> 105 us  [on_device(): pl.pallas_call(kernel, out_shape=[jax.ShapeDtypeStruct((DSH, FF), BF16),...]
where the time goes in v4:
time: 112 us
  Pallas kernels  105 us (94%)
  local copies, waits for them, and re-layouts  5.46 us (5%)
  between operations  1.3 us (1%)
    pallas_call x1, Pallas kernels, on_device(): pl.pallas_call(kernel, out_shape=[jax.ShapeDtypeStruct((DSH, FF), BF16),...  105 us
    unnamed x7, local copies, waits for them, and re-layouts  5.46 us

profile of v4, /device:TPU:1, one launch (start us, length us, event | category | flops | bytes accessed | tf_op | source)
XLA Modules:
  0.0 112.1 jit_solution(12136523589739909230)
XLA Ops:
  1.3 105.3 %window.1 = (bf16[384,3072]{1,0:T(8,128)(2,1)}, bf16[768,1536]{1,0:T(8,128)(2,1)}, f32[31,1536]{1,0:T(8,128)}) custom-call(s32[1,1]{1,0:T(1,128)S(6)} %copy.16.count_in, s32[1,48]{1,0:T(1,128)} %bitcast.9, s32[1,64]{1,0:T(1,128)} %order_in.1, bf16[48,64,128]{2,1,0:T(8,128)(2,1)} %bitcast.7, f32[31,1536]{1,0:T(8,128)} %taps.1, f32[1536]{0:T(1024)} %gain.1, ...), custom_call_target="tpu_custom_call" | custom-call | tf_op jit(solution)/shard_map/window/pallas_call | solution.py:620
  106.6 0.0 copy-start
  106.6 3.4 %copy.17 = bf16[1,384,3072]{2,1,0:T(8,128)(2,1)} copy(bf16[1,384,3072]{2,1,0:T(8,128)(2,1)} %bitcast.6) | data formatting | bytes 4718592
  110.0 0.0 copy-done
  110.0 0.0 copy-start.1
  110.0 1.4 %copy.18 = bf16[1,768,1536]{2,1,0:T(8,128)(2,1)} copy(bf16[1,768,1536]{2,1,0:T(8,128)(2,1)S(1)} %bitcast.5) | data formatting | bytes 4718592
  111.4 0.0 copy-done.1
  111.4 0.7 copy.19
Async XLA Ops:
  106.6 3.4 %copy-start = (bf16[768,1536]{1,0:T(8,128)(2,1)S(1)}, bf16[768,1536]{1,0:T(8,128)(2,1)}, u32[]{:S(2)}) copy-start(bf16[768,1536]{1,0:T(8,128)(2,1)} %get-tuple-element.7) | copy-start | bytes 7077892
  110.0 1.4 %copy-start.1 = (f32[31,1536]{1,0:T(8,128)S(1)}, f32[31,1536]{1,0:T(8,128)}, u32[]{:S(2)}) copy-start(f32[31,1536]{1,0:T(8,128)} %get-tuple-element.14) | copy-start | bytes 571396

commit v5 on v4

--- a/solution.py
+++ b/solution.py
@@ -239,7 +239,7 @@
         return frames[jnp.minimum(lax.rem(inv[j, 0] - start + NDP * NH, NDP), NH - 1)]
 
     def send(k, carry):
-        kk = lax.rem(k * 27, NDP)
+        kk = lax.rem(k * 37, NDP)
         to = lax.rem(dp + kk, NDP)
         sbuf[to] = pick_home(to)
         remote(sbuf.at[to], rbuf.at[kk], as_, ar, (to, f)).start()
@@ -539,6 +539,10 @@
     cot_sib.wait()
     masked[pl.ds(3 * ROWS, ROWS), :] = turned(3)
     hidden_grads(1)
+    r2[0] = s1[...]
+    all_here(r2, 1)
+    s2[...] = ordered(r2, far)
+    spread(three)
     for g in range(4):
         if g == 2:
             norm_here(1, 2 * ROWS)
@@ -546,10 +550,6 @@
             group(1)
         span = pl.ds(g * ROWS, ROWS)
         masked[span, :] = jnp.where(maskv[g][:, :1] > 0, masked[span, :].astype(F32), 0.0).astype(BF16)
-    r2[0] = s1[...]
-    all_here(r2, 1)
-    s2[...] = ordered(r2, far)
-    spread(three)
 
     def gin_tile(i, n):
         return jnp.dot(

time: 112 us -> 112 us (level)
  no operation moved by 1% of the time
where the time goes in v5:
time: 112 us
  Pallas kernels  105 us (94%)
  local copies, waits for them, and re-layouts  5.46 us (5%)
  between operations  1.3 us (1%)
    pallas_call x1, Pallas kernels, on_device(): pl.pallas_call(kernel, out_shape=[jax.ShapeDtypeStruct((DSH, FF), BF16),...  105 us
    unnamed x7, local copies, waits for them, and re-layouts  5.46 us

profile of v5, /device:TPU:1, one launch (start us, length us, event | category | flops | bytes accessed | tf_op | source)
XLA Modules:
  0.0 112.0 jit_solution(14448842323099317198)
XLA Ops:
  1.3 105.2 %window.1 = (bf16[384,3072]{1,0:T(8,128)(2,1)}, bf16[768,1536]{1,0:T(8,128)(2,1)}, f32[31,1536]{1,0:T(8,128)}) custom-call(s32[1,1]{1,0:T(1,128)S(6)} %copy.16.count_in, s32[1,48]{1,0:T(1,128)} %bitcast.9, s32[1,64]{1,0:T(1,128)} %order_in.1, bf16[48,64,128]{2,1,0:T(8,128)(2,1)} %bitcast.7, f32[31,1536]{1,0:T(8,128)} %taps.1, f32[1536]{0:T(1024)} %gain.1, ...), custom_call_target="tpu_custom_call" | custom-call | tf_op jit(solution)/shard_map/window/pallas_call | solution.py:620
  106.5 0.0 copy-start
  106.5 3.4 %copy.17 = bf16[1,384,3072]{2,1,0:T(8,128)(2,1)} copy(bf16[1,384,3072]{2,1,0:T(8,128)(2,1)} %bitcast.6) | data formatting | bytes 4718592
  109.9 0.0 copy-done
  109.9 0.0 copy-start.1
  109.9 1.4 %copy.18 = bf16[1,768,1536]{2,1,0:T(8,128)(2,1)} copy(bf16[1,768,1536]{2,1,0:T(8,128)(2,1)S(1)} %bitcast.5) | data formatting | bytes 4718592
  111.3 0.0 copy-done.1
  111.3 0.7 copy.19
Async XLA Ops:
  106.5 3.4 %copy-start = (bf16[768,1536]{1,0:T(8,128)(2,1)S(1)}, bf16[768,1536]{1,0:T(8,128)(2,1)}, u32[]{:S(2)}) copy-start(bf16[768,1536]{1,0:T(8,128)(2,1)} %get-tuple-element.7) | copy-start | bytes 7077892
  109.9 1.4 %copy-start.1 = (f32[31,1536]{1,0:T(8,128)S(1)}, f32[31,1536]{1,0:T(8,128)}, u32[]{:S(2)}) copy-start(f32[31,1536]{1,0:T(8,128)} %get-tuple-element.14) | copy-start | bytes 571396
